TPU v7x, 128 devices: a whole 4x4x4 slice. The times are simulated.
128 devices in a mesh: patch: 4 (over x_hi, core), epoch: 32 (over z, x_lo, y).
Axes of the slice: x: 4 (x_hi: 2, x_lo: 2; x = x_hi * 2 + x_lo), y: 4, z: 4, core: 2. Of those that a mesh axis runs over, the one named last changes fastest.
Arguments:
- images: bfloat16 [384, 512, 4096], P('epoch', None, 'patch'), may hold values from -8 to 8
- counts: int32 [4, 32], P('patch', 'epoch'), may hold values from 1 to 12, as said below
- slot_weight: float32 [4, 384], P('patch', 'epoch'), may hold values from 0.2 to 5
- kernel_index: int32 [4, 384, 3], P('patch', 'epoch'), may hold values from 0 to 7
- kernel_slope: float32 [4, 384], P('patch', 'epoch'), may hold values from -1 to 1
- tap_basis: float32 [8, 21], replicated, may hold values from 0 to 0.1
Outputs:
- template: bfloat16 [512, 4096], P(None, 'patch')
- differences: bfloat16 [384, 512, 4096], P('epoch', None, 'patch')
Inputs may be any that keep to these rules, and one draw needn't show every extreme that they name: `counts`: slots e with e mod 12 >= the holder's count are empty; in every patch some holder uses all 12 slots.
All inputs are finite; a program needn't handle non-finite values.
Results may differ from a plain program's by a relative error of at most 0.0022.
Values may be sent and summed in bfloat16 or wider, within the bound.
No kernel may reach another device: no remote copies, remote signals or barrier semaphores. Data moves between devices by JAX's collectives and lax.ppermute only.
A program may use at most 128 MiB of HBM per device.

v0:
```python
import functools

import jax
import jax.numpy as jnp
from jax import lax
from jax.experimental import pallas as pl
from jax.experimental.pallas import tpu as pltpu
from jax.sharding import PartitionSpec as P

f32 = jnp.float32
bf16 = jnp.bfloat16
LANE = 128
STEPS = 32767.0
WEIGHT_STEPS = 2.0**17
PAD = 16
VMEM_LIMIT = 44 * 2**20


def smem():
    return pl.BlockSpec(memory_space=pltpu.SMEM)


def vmem():
    return pl.BlockSpec(memory_space=pltpu.VMEM)


def params():
    return pltpu.CompilerParams(vmem_limit_bytes=VMEM_LIMIT)


def bands_kernel(index_ref, basis_ref, vert_ref, horiz_ref, *, slots, taps):
    lead = PAD - taps // 2
    lane = lax.broadcasted_iota(jnp.int32, (8, 2 * LANE), 1)

    def body(s, _):
        first, second, third = index_ref[s, 0], index_ref[s, 1], index_ref[s, 2]
        row0 = jnp.zeros((8, 2 * LANE), f32)
        row1 = jnp.zeros((8, 2 * LANE), f32)
        row2 = jnp.zeros((8, 2 * LANE), f32)
        for t in range(taps):
            row0 = jnp.where(lane == lead + t, basis_ref[first, t], row0)
            back = lane == 2 * LANE - lead - t
            row1 = jnp.where(back, basis_ref[second, t], row1)
            row2 = jnp.where(back, basis_ref[third, t], row2)
        row2 = jnp.concatenate([row2[:, LANE:], row2[:, :LANE]], axis=1)
        for base in range(0, 2 * LANE, 16):
            if base < LANE:
                halves = [pltpu.roll(row0, base + 8 * h, 1, stride=1, stride_axis=0) for h in range(2)]
                vert_ref[s, base : base + 16, :] = jnp.concatenate(halves, axis=0).astype(bf16)
            halves = []
            for h in range(2):
                r1 = pltpu.roll(row1, base + 8 * h, 1, stride=1, stride_axis=0)
                r2 = pltpu.roll(row2, base + 8 * h, 1, stride=1, stride_axis=0)
                halves.append(jnp.concatenate([r1[:, :LANE], r2[:, LANE:]], axis=1))
            horiz_ref[s, base : base + 16, :] = jnp.concatenate(halves, axis=0).astype(bf16)
        return 0

    lax.fori_loop(0, slots, body, 0)


def tap_bands(index, basis):
    slots = index.shape[0]
    return pl.pallas_call(
        functools.partial(bands_kernel, slots=slots, taps=basis.shape[1]),
        out_shape=(
            jax.ShapeDtypeStruct((slots, LANE, 2 * LANE), bf16),
            jax.ShapeDtypeStruct((slots, 2 * LANE, 2 * LANE), bf16),
        ),
        in_specs=[smem(), smem()],
        out_specs=(vmem(), vmem()),
        compiler_params=params(),
        name="tap_bands",
    )(index, basis)


def pack(parts, weight_word, out_ref, base):
    top = jnp.abs(parts[0])
    for part in parts[1:]:
        top = jnp.maximum(top, jnp.abs(part))
    exponent = jnp.ceil(jnp.log2(jnp.maximum(top, 1e-30)) + 0.002)
    factor = STEPS / jnp.exp2(exponent)
    words = [jnp.round(part * factor).astype(jnp.int32) for part in parts]
    half = len(parts) // 2
    for i in range(half):
        out_ref[base + 8 * i : base + 8 * i + 8, :] = (words[half + i] << 16) | (words[i] & 0xFFFF)
    out_ref[base + 8 * half : base + 8 * half + 8, :] = weight_word + (exponent.astype(jnp.int32) + 128)


def accumulate_kernel(count_ref, weight_ref, image_ref, out_ref, held, arrived, *, chunk):
    slots, rows, width = image_ref.shape
    blocks, _, block, _ = held.shape
    copies = [
        pltpu.make_async_copy(image_ref.at[:, n * block : (n + 1) * block, :], held.at[n], arrived.at[n])
        for n in range(blocks)
    ]
    for copy in copies:
        copy.start()
    weights = [jnp.where(s < count_ref[0, 0], weight_ref[0, s], 0.0) for s in range(slots)]
    total = weights[0]
    for s in range(1, slots):
        total = total + weights[s]
    weight_word = jnp.round(jnp.full((8, LANE), total, f32) * WEIGHT_STEPS).astype(jnp.int32) << 8
    cols = width // LANE
    stride = (cols + 1) * 8
    for n, copy in enumerate(copies):
        copy.wait()
        for q in range(block // chunk):
            upper, lower = [], []
            for c in range(cols):
                at = slice(c * LANE, (c + 1) * LANE)
                here = slice(q * chunk, (q + 1) * chunk)
                part = held[n, 0, here, at].astype(f32) * weights[0]
                for s in range(1, slots):
                    part = part + held[n, s, here, at].astype(f32) * weights[s]
                upper.append(part[:8])
                lower.append(part[8:])
            pack(upper + lower, weight_word, out_ref, (n * (block // chunk) + q) * stride)


def accumulate(counts, weight, images, chunk=16, block=64):
    slots, rows, width = images.shape
    return pl.pallas_call(
        functools.partial(accumulate_kernel, chunk=chunk),
        out_shape=jax.ShapeDtypeStruct((rows // chunk * (width // LANE + 1) * 8, LANE), jnp.int32),
        in_specs=[smem(), smem(), pl.BlockSpec(memory_space=pl.ANY)],
        out_specs=vmem(),
        scratch_shapes=[
            pltpu.VMEM((rows // block, slots, block, width), bf16),
            pltpu.SemaphoreType.DMA((rows // block,)),
        ],
        compiler_params=params(),
        name="accumulate",
    )(counts, weight, images)


def share_kernel(piece_ref, own_ref, first_ref, last_ref):
    parts = piece_ref.shape[0]
    cols = own_ref.shape[1] // LANE
    upper, lower, weight = [None] * cols, [None] * cols, None
    for p in range(parts):
        meta = piece_ref[p, 8 * cols :, :]
        weight = meta >> 8 if weight is None else weight + (meta >> 8)
        scale = jnp.exp2(((meta & 0xFF) - 128).astype(f32)) / STEPS
        for c in range(cols):
            word = piece_ref[p, 8 * c : 8 * c + 8, :]
            up = ((word << 16) >> 16).astype(f32) * scale
            low = (word >> 16).astype(f32) * scale
            upper[c] = up if p == 0 else upper[c] + up
            lower[c] = low if p == 0 else lower[c] + low
    weight = weight.astype(f32) / WEIGHT_STEPS
    for c in range(cols):
        block = jnp.concatenate([upper[c] / weight, lower[c] / weight], axis=0).astype(bf16)
        own_ref[:, c * LANE : (c + 1) * LANE] = block
        if c == 0:
            first_ref[...] = block
        if c == cols - 1:
            last_ref[...] = block


def share(pieces, chunk, width):
    return pl.pallas_call(
        share_kernel,
        out_shape=(
            jax.ShapeDtypeStruct((chunk, width), bf16),
            jax.ShapeDtypeStruct((chunk, LANE), bf16),
            jax.ShapeDtypeStruct((chunk, LANE), bf16),
        ),
        in_specs=[vmem()],
        out_specs=(vmem(), vmem(), vmem()),
        compiler_params=params(),
        name="share",
    )(pieces)


def widen_kernel(own_ref, low_ref, high_ref, out_ref, *, parts):
    rows, width = own_ref.shape
    cols = width // LANE
    lane = lax.broadcasted_iota(jnp.int32, (rows, LANE), 1)
    before = pltpu.roll(low_ref[...].astype(f32), PAD, 1)
    for c in range(cols + 1):
        here = own_ref[:, c * LANE : (c + 1) * LANE] if c < cols else high_ref[...]
        here = pltpu.roll(here.astype(f32), PAD, 1)
        block = jnp.where(lane < PAD, before, here).astype(bf16)
        for p in range(parts):
            out_ref[p, :, c * LANE : (c + 1) * LANE] = block
        before = here


def widen(own, low, high, parts):
    rows, width = own.shape
    return pl.pallas_call(
        functools.partial(widen_kernel, parts=parts),
        out_shape=jax.ShapeDtypeStruct((parts, rows, width + LANE), bf16),
        in_specs=[vmem()] * 3,
        out_specs=vmem(),
        compiler_params=params(),
        name="widen",
    )(own, low, high)


def match_kernel(
    count_ref, slope_ref, wide_ref, vert_ref, horiz_ref, image_ref, diff_ref, template_ref, padded, vertical, *, group
):
    step = pl.program_id(0)
    rows, width = image_ref.shape[1:]
    cols = width // LANE
    count = count_ref[0, 0]

    @pl.when(step == 0)
    def _():
        padded[0:PAD, :] = jnp.zeros((PAD, width + LANE), bf16)
        padded[PAD + rows :, :] = jnp.zeros((LANE - PAD, width + LANE), bf16)
        padded[PAD : PAD + rows, :] = wide_ref[...]

    @pl.when(step < rows // LANE)
    def _():
        lane = lax.broadcasted_iota(jnp.int32, (LANE, LANE), 1)
        at = pl.ds(pl.multiple_of(step * LANE, LANE), LANE)
        here = pltpu.roll(wide_ref[at, :LANE].astype(f32), LANE - PAD, 1)
        for c in range(cols):
            after = pltpu.roll(wide_ref[at, (c + 1) * LANE : (c + 2) * LANE].astype(f32), LANE - PAD, 1)
            template_ref[:, c * LANE : (c + 1) * LANE] = jnp.where(lane < LANE - PAD, here, after).astype(bf16)
            here = after

    @pl.when(step * group < count)
    def _():
        band = vert_ref[...].reshape(group * LANE, 2 * LANE)
        for n in range(rows // LANE):
            for j in range(0, cols + 1, 2):
                at = slice(j * LANE, min(j + 2, cols + 1) * LANE)
                part = jnp.dot(band, padded[n * LANE : (n + 2) * LANE, at], preferred_element_type=f32).astype(bf16)
                for g in range(group):
                    vertical[g, n * LANE : (n + 1) * LANE, at] = part[g * LANE : (g + 1) * LANE]
        start = lax.axis_index("patch") * width
        center = width * lax.axis_size("patch") / 2
        column = lax.broadcasted_iota(jnp.int32, (8, LANE), 1) + start
        for g in range(group):
            slot = step * group + g
            live = slot < count
            slope = slope_ref[0, slot]
            for m in range(cols):
                at = slice(m * LANE, (m + 1) * LANE)
                position = ((column + m * LANE).astype(f32) + 0.5 - center) / center
                factor = (slope * position)[0:1]
                both = jnp.dot(vertical[g, :, m * LANE : (m + 2) * LANE], horiz_ref[g], preferred_element_type=f32)
                matched = both[:, :LANE] + factor * both[:, LANE:]
                result = jnp.where(live, image_ref[g, :, at].astype(f32) - matched, 0.0)
                diff_ref[g, :, at] = result.astype(bf16)

    @pl.when(step * group >= count)
    def _():
        diff_ref[...] = jnp.zeros(diff_ref.shape, bf16)


def match(counts, slopes, wide, vert, horiz, images, group=2):
    slots, rows, width = images.shape
    last = rows // LANE - 1
    return pl.pallas_call(
        functools.partial(match_kernel, group=group),
        grid=(slots // group,),
        out_shape=(jax.ShapeDtypeStruct(images.shape, bf16), jax.ShapeDtypeStruct((rows, width), bf16)),
        in_specs=[
            smem(),
            smem(),
            vmem(),
            pl.BlockSpec((group, LANE, 2 * LANE), lambda i: (i, 0, 0)),
            pl.BlockSpec((group, 2 * LANE, 2 * LANE), lambda i: (i, 0, 0)),
            pl.BlockSpec((group, rows, width), lambda i: (i, 0, 0)),
        ],
        out_specs=(
            pl.BlockSpec((group, rows, width), lambda i: (i, 0, 0)),
            pl.BlockSpec((LANE, width), lambda i: (jnp.minimum(i, last), 0)),
        ),
        scratch_shapes=[
            pltpu.VMEM((rows + LANE, width + LANE), bf16),
            pltpu.VMEM((group, rows, width + LANE), bf16),
        ],
        compiler_params=params(),
        name="match",
    )(counts, slopes, wide, vert, horiz, images)


def on_device(images, counts, slot_weight, kernel_index, kernel_slope, tap_basis):
    slots, rows, width = images.shape
    parts = lax.axis_size("epoch")
    patches = lax.axis_size("patch")
    chunk = rows // parts
    partial = accumulate(counts, slot_weight, images, chunk)
    pieces = lax.all_to_all(partial, "epoch", 0, 0, tiled=True)
    own, first, last = share(pieces.reshape(parts, -1, LANE), chunk, width)
    low = lax.ppermute(last, "patch", [(i, i + 1) for i in range(patches - 1)])
    high = lax.ppermute(first, "patch", [(i + 1, i) for i in range(patches - 1)])
    vert, horiz = tap_bands(kernel_index[0], tap_basis)
    copies = widen(own, low, high, parts)
    wide = lax.all_to_all(copies, "epoch", 0, 0, tiled=True).reshape(rows, width + LANE)
    differences, template = match(counts, kernel_slope, wide, vert, horiz, images)
    return (template, differences)


def solution(mesh):
    in_specs = (
        P("epoch", None, "patch"),
        P("patch", "epoch"),
        P("patch", "epoch"),
        P("patch", "epoch", None),
        P("patch", "epoch"),
        P(),
    )
    out_specs = (P(None, "patch"), P("epoch", None, "patch"))
    return jax.shard_map(
        on_device, mesh=mesh, in_specs=in_specs, out_specs=out_specs, check_vma=False
    )
```

profile of v0, /device:TPU:1, one launch (start us, length us, event | category | flops | bytes accessed | tf_op | source)
XLA Modules:
  0.0 84.4 jit_solution(5235225239735963473)
XLA Ops:
  1.3 0.0 copy-start.1
  1.3 0.6 copy-done.1
  1.9 5.6 %accumulate.1 = s32[2304,128]{1,0:T(8,128)S(1)} custom-call(s32[1,1]{1,0:T(1,128)S(6)} %copy.10.count_ref, f32[1,12]{1,0:T(1,128)S(1)} %copy-done.1, bf16[12,512,1024]{2,1,0:T(8,128)(2,1)} %image_ref.3), custom_call_target="tpu_custom_call" | custom-call | tf_op jit(solution)/shard_map/accumulate/pallas_call | solution.py:122
  7.6 27.6 %all_to_all.14.piece_ref = s32[32,72,128]{2,1,0:T(8,128)S(1)} all-to-all(s32[32,72,128]{2,1,0:T(8,128)S(1)} %bitcast.4), channel_id=1, replica_groups=mesh['patch'=4,'epoch'=32] {'epoch'}, dimensions={0} | all-to-all | bytes 2359296 | tf_op jit(solution)/shard_map/all_to_all | solution.py:289
  35.1 0.4 share.1
  35.5 6.6 %collective-permute-start = (bf16[16,128]{1,0:T(8,128)(2,1)S(1)}, bf16[16,128]{1,0:T(8,128)(2,1)S(1)}, u32[]{:S(2)}, u32[]{:S(2)}) collective-permute-start(bf16[16,128]{1,0:T(8,128)(2,1)S(1)} %get-tuple-element.10), channel_id=1, source_target_pairs={{0,32},{32,64},{64,96},{1,33},{33,65},{65,97},{2,34},{34,66},{66,9... | collective-permute-start | bytes 12296 | tf_op jit(solution)/shard_map/ppermute | solution.py:291
  42.1 1.9 %collective-permute-start.1 = (bf16[16,128]{1,0:T(8,128)(2,1)S(1)}, bf16[16,128]{1,0:T(8,128)(2,1)S(1)}, u32[]{:S(2)}, u32[]{:S(2)}) collective-permute-start(bf16[16,128]{1,0:T(8,128)(2,1)S(1)} %get-tuple-element.11), channel_id=1, source_target_pairs={{32,0},{64,32},{96,64},{33,1},{65,33},{97,65},{34,2},{66,34},{98,6... | collective-permute-start | bytes 12296 | tf_op jit(solution)/shard_map/ppermute | solution.py:292
  44.1 0.0 collective-permute-done.low_ref
  44.1 4.5 %collective-permute-done.1.high_ref = bf16[16,128]{1,0:T(8,128)(2,1)S(1)} collective-permute-done((bf16[16,128]{1,0:T(8,128)(2,1)S(1)}, bf16[16,128]{1,0:T(8,128)(2,1)S(1)}, u32[]{:S(2)}, u32[]{:S(2)}) %collective-permute-start.1) | collective-permute-done | bytes 4128 | tf_op jit(solution)/shard_map/ppermute | solution.py:292
  48.6 1.2 %widen.1 = bf16[32,16,1152]{2,1,0:T(8,128)(2,1)} custom-call(bf16[16,1024]{1,0:T(8,128)(2,1)S(1)} %get-tuple-element.9.own_ref, bf16[16,128]{1,0:T(8,128)(2,1)S(1)} %collective-permute-done.low_ref, bf16[16,128]{1,0:T(8,128)(2,1)S(1)} %collective-permute-done.1.high_ref), custom_call_target="tpu_custom_call" | custom-call | tf_op jit(solution)/shard_map/widen/pallas_call | solution.py:191
  49.8 0.0 copy-start.3
  49.8 0.0 copy-start
  49.8 0.0 copy-start.2
  49.8 4.1 %all-to-all-start.1 = ((bf16[32,16,1152]{2,1,0:T(8,128)(2,1)}), bf16[32,16,1152]{2,1,0:T(8,128)(2,1)S(1)}, u32[]{:S(2)}, u32[]{:S(2)}) async-start(bf16[32,16,1152]{2,1,0:T(8,128)(2,1)} %widen.1), calls=%async_computation.1 | async-start | bytes 2359296 | tf_op jit(solution)/shard_map/all_to_all | solution.py:295
  53.9 0.0 copy-done.3
  53.9 0.1 copy.9
  54.0 0.0 copy-done
  54.0 2.5 %tap_bands.1 = (bf16[12,128,256]{2,1,0:T(8,128)(2,1)S(1)}, bf16[12,256,256]{2,1,0:T(8,128)(2,1)S(1)}) custom-call(s32[12,3]{1,0:T(8,128)S(1)} %bitcast.5, f32[8,21]{1,0:T(8,128)S(1)} %copy-done), custom_call_target="tpu_custom_call" | custom-call | tf_op jit(solution)/shard_map/tap_bands/pallas_call | solution.py:63
  56.5 12.5 %all-to-all-done.1 = bf16[32,16,1152]{2,1,0:T(8,128)(2,1)S(1)} async-done(((bf16[32,16,1152]{2,1,0:T(8,128)(2,1)}), bf16[32,16,1152]{2,1,0:T(8,128)(2,1)S(1)}, u32[]{:S(2)}, u32[]{:S(2)}) %all-to-all-start.1) | async-done | bytes 1179680 | tf_op jit(solution)/shard_map/all_to_all | solution.py:295
  69.0 0.0 copy-done.2
  69.0 15.4 %match.1 = (bf16[12,512,1024]{2,1,0:T(8,128)(2,1)}, bf16[512,1024]{1,0:T(8,128)(2,1)}) custom-call(s32[1,1]{1,0:T(1,128)S(6)} %copy.10.count_ref, f32[1,12]{1,0:T(1,128)S(1)} %copy-done.2, bf16[512,1152]{1,0:T(8,128)(2,1)S(1)} %bitcast.3, bf16[12,128,256]{2,1,0:T(8,128)(2,1)S(1)} %get-tuple-element.12.vert_ref, ...), custom_call_target="tpu_custom_call" | custom-call | tf_op jit(solution)/shard_map/match/pallas_call | solution.py:258
Async XLA Ops:
  1.3 0.7 copy-start.1
  35.5 8.5 %collective-permute-start = (bf16[16,128]{1,0:T(8,128)(2,1)S(1)}, bf16[16,128]{1,0:T(8,128)(2,1)S(1)}, u32[]{:S(2)}, u32[]{:S(2)}) collective-permute-start(bf16[16,128]{1,0:T(8,128)(2,1)S(1)} %get-tuple-element.10), channel_id=1, source_target_pairs={{0,32},{32,64},{64,96},{1,33},{33,65},{65,97},{2,34},{34,66},{66,9... | collective-permute-start | bytes 12296 | tf_op jit(solution)/shard_map/ppermute | solution.py:291
  42.1 6.4 %collective-permute-start.1 = (bf16[16,128]{1,0:T(8,128)(2,1)S(1)}, bf16[16,128]{1,0:T(8,128)(2,1)S(1)}, u32[]{:S(2)}, u32[]{:S(2)}) collective-permute-start(bf16[16,128]{1,0:T(8,128)(2,1)S(1)} %get-tuple-element.11), channel_id=1, source_target_pairs={{32,0},{64,32},{96,64},{33,1},{65,33},{97,65},{34,2},{66,34},{98,6... | collective-permute-start | bytes 12296 | tf_op jit(solution)/shard_map/ppermute | solution.py:292
  49.8 4.1 %copy-start.3 = (s32[1,12,3]{1,0,2:T(1,128)S(1)}, s32[1,12,3]{1,0,2:T(1,128)}, u32[]{:S(2)}) copy-start(s32[1,12,3]{1,0,2:T(1,128)} %param.9) | copy-start | bytes 436
  49.8 4.2 %copy-start = (f32[8,21]{1,0:T(8,128)S(1)}, f32[8,21]{1,0:T(8,128)}, u32[]{:S(2)}) copy-start(f32[8,21]{1,0:T(8,128)} %basis_ref.1) | copy-start | bytes 2020
  49.8 19.2 %copy-start.2 = (f32[1,12]{1,0:T(1,128)S(1)}, f32[1,12]{1,0:T(1,128)}, u32[]{:S(2)}) copy-start(f32[1,12]{1,0:T(1,128)} %slope_ref.1) | copy-start | bytes 148
  49.8 19.2 %all-to-all-start.1 = ((bf16[32,16,1152]{2,1,0:T(8,128)(2,1)}), bf16[32,16,1152]{2,1,0:T(8,128)(2,1)S(1)}, u32[]{:S(2)}, u32[]{:S(2)}) async-start(bf16[32,16,1152]{2,1,0:T(8,128)(2,1)} %widen.1), calls=%async_computation.1 | async-start | bytes 2359296 | tf_op jit(solution)/shard_map/all_to_all | solution.py:295
where the time goes:
time: 84.9 us; the launch traced here: 84.4 us
  blocking collectives  27.6 us (33%)
  Pallas kernels  25.2 us (30%)
  waiting for transfers between devices  17 us (20%)
  starting transfers between devices  12.6 us (15%)
  between operations  1.35 us (2%)
    all_to_all x1, blocking collectives, on_device(): pieces = lax.all_to_all(partial, 'epoch', 0, 0, tiled=True)  27.6 us
    pallas_call x1, Pallas kernels, match(): pl.pallas_call(functools.partial(match_kernel, group=group), grid=(slots...  15.4 us
    all_to_all x1, waiting for transfers between devices, on_device(): lax.all_to_all(copies, 'epoch', 0, 0, tiled=True)  12.5 us
    ppermute x1, starting transfers between devices, on_device(): low = lax.ppermute(last, 'patch', [(i, i + 1) for i in range(patches - 1)])  6.59 us
    pallas_call x1, Pallas kernels, accumulate(): pl.pallas_call(functools.partial(accumulate_kernel, chunk=chunk), out_sha...  5.62 us
    ppermute x1, waiting for transfers between devices, on_device(): lax.ppermute(first, 'patch', [(i + 1, i) for i in range(patches - 1)])  4.49 us
    all_to_all x1, starting transfers between devices, on_device(): lax.all_to_all(copies, 'epoch', 0, 0, tiled=True)  4.07 us
    pallas_call x1, Pallas kernels, tap_bands(): pl.pallas_call(functools.partial(bands_kernel, slots=slots, taps=basis.sh...  2.54 us
  transfers between devices with their start and end apart: 3, of which 2 were waited for; matrix products, arithmetic and copies ran while one was open for 0% of the time, Pallas kernels for 3%

commit v1 on v0

v1 whole, which is shorter than its diff:
```python
import functools

import jax
import jax.numpy as jnp
from jax import lax
from jax.experimental import pallas as pl
from jax.experimental.pallas import tpu as pltpu
from jax.sharding import PartitionSpec as P

f32 = jnp.float32
bf16 = jnp.bfloat16
LANE = 128
STEPS = 32767.0
WEIGHT_STEPS = 2.0**17
PAD = 16
VMEM_LIMIT = 50 * 2**20
GROUP = 2


def smem():
    return pl.BlockSpec(memory_space=pltpu.SMEM)


def vmem():
    return pl.BlockSpec(memory_space=pltpu.VMEM)


def params():
    return pltpu.CompilerParams(vmem_limit_bytes=VMEM_LIMIT)


def bands_kernel(basis_ref, vert_ref, horiz_ref):
    profiles, taps = basis_ref.shape
    lead = PAD - taps // 2
    lane = lax.broadcasted_iota(jnp.int32, (8, 2 * LANE), 1)

    def body(b, _):
        down = jnp.zeros((8, 2 * LANE), f32)
        across = jnp.zeros((8, 2 * LANE), f32)
        for t in range(taps):
            down = jnp.where(lane == lead + t, basis_ref[b, t], down)
            across = jnp.where(lane == 2 * LANE - lead - t, basis_ref[b, t], across)
        for base in range(0, 2 * LANE, 16):
            if base < LANE:
                halves = [pltpu.roll(down, base + 8 * h, 1, stride=1, stride_axis=0) for h in range(2)]
                vert_ref[b, base : base + 16, :] = jnp.concatenate(halves, axis=0).astype(bf16)
            halves = [pltpu.roll(across, base + 8 * h, 1, stride=1, stride_axis=0) for h in range(2)]
            horiz_ref[b, base : base + 16, :] = jnp.concatenate(halves, axis=0)[:, :LANE].astype(bf16)
        return 0

    lax.fori_loop(0, profiles, body, 0)


def tap_bands(basis):
    profiles = basis.shape[0]
    return pl.pallas_call(
        bands_kernel,
        out_shape=(
            jax.ShapeDtypeStruct((profiles, LANE, 2 * LANE), bf16),
            jax.ShapeDtypeStruct((profiles, 2 * LANE, LANE), bf16),
        ),
        in_specs=[smem()],
        out_specs=(vmem(), vmem()),
        compiler_params=params(),
        name="tap_bands",
    )(basis)


def pack(parts, weight_word, out_ref, base):
    top = jnp.abs(parts[0])
    for part in parts[1:]:
        top = jnp.maximum(top, jnp.abs(part))
    exponent = jnp.ceil(jnp.log2(jnp.maximum(top, 1e-30)) + 0.002)
    factor = STEPS / jnp.exp2(exponent)
    words = [jnp.round(part * factor).astype(jnp.int32) for part in parts]
    half = len(parts) // 2
    for i in range(half):
        out_ref[base + 8 * i : base + 8 * i + 8, :] = (words[half + i] << 16) | (words[i] & 0xFFFF)
    out_ref[base + 8 * half : base + 8 * half + 8, :] = weight_word + (exponent.astype(jnp.int32) + 128)


def accumulate_kernel(count_ref, weight_ref, image_ref, out_ref, held, arrived, *, chunk):
    slots, rows, width = image_ref.shape
    blocks, _, block, _ = held.shape
    copies = [
        pltpu.make_async_copy(image_ref.at[:, n * block : (n + 1) * block, :], held.at[n], arrived.at[n])
        for n in range(blocks)
    ]
    for copy in copies:
        copy.start()
    weights = [jnp.where(s < count_ref[0, 0], weight_ref[0, s], 0.0) for s in range(slots)]
    total = weights[0]
    for s in range(1, slots):
        total = total + weights[s]
    weight_word = jnp.round(jnp.full((8, LANE), total, f32) * WEIGHT_STEPS).astype(jnp.int32) << 8
    cols = width // LANE
    stride = (cols + 1) * 8
    for n, copy in enumerate(copies):
        copy.wait()
        for q in range(block // chunk):
            upper, lower = [], []
            for c in range(cols):
                at = slice(c * LANE, (c + 1) * LANE)
                here = slice(q * chunk, (q + 1) * chunk)
                part = held[n, 0, here, at].astype(f32) * weights[0]
                for s in range(1, slots):
                    part = part + held[n, s, here, at].astype(f32) * weights[s]
                upper.append(part[:8])
                lower.append(part[8:])
            pack(upper + lower, weight_word, out_ref, (n * (block // chunk) + q) * stride)


def accumulate(counts, weight, images, chunk=16, block=64):
    slots, rows, width = images.shape
    return pl.pallas_call(
        functools.partial(accumulate_kernel, chunk=chunk),
        out_shape=jax.ShapeDtypeStruct((rows // chunk * (width // LANE + 1) * 8, LANE), jnp.int32),
        in_specs=[smem(), smem(), pl.BlockSpec(memory_space=pl.ANY)],
        out_specs=vmem(),
        scratch_shapes=[
            pltpu.VMEM((rows // block, slots, block, width), bf16),
            pltpu.SemaphoreType.DMA((rows // block,)),
        ],
        compiler_params=params(),
        name="accumulate",
    )(counts, weight, images)


def share_kernel(piece_ref, own_ref, first_ref, last_ref):
    parts = piece_ref.shape[0]
    cols = own_ref.shape[1] // LANE
    upper, lower, weight = [None] * cols, [None] * cols, None
    for p in range(parts):
        meta = piece_ref[p, 8 * cols :, :]
        weight = meta >> 8 if weight is None else weight + (meta >> 8)
        scale = jnp.exp2(((meta & 0xFF) - 128).astype(f32)) / STEPS
        for c in range(cols):
            word = piece_ref[p, 8 * c : 8 * c + 8, :]
            up = ((word << 16) >> 16).astype(f32) * scale
            low = (word >> 16).astype(f32) * scale
            upper[c] = up if p == 0 else upper[c] + up
            lower[c] = low if p == 0 else lower[c] + low
    weight = weight.astype(f32) / WEIGHT_STEPS
    for c in range(cols):
        block = jnp.concatenate([upper[c] / weight, lower[c] / weight], axis=0).astype(bf16)
        own_ref[:, c * LANE : (c + 1) * LANE] = block
        if c == 0:
            first_ref[...] = block
        if c == cols - 1:
            last_ref[...] = block


def share(pieces, chunk, width):
    return pl.pallas_call(
        share_kernel,
        out_shape=(
            jax.ShapeDtypeStruct((chunk, width), bf16),
            jax.ShapeDtypeStruct((chunk, LANE), bf16),
            jax.ShapeDtypeStruct((chunk, LANE), bf16),
        ),
        in_specs=[vmem()],
        out_specs=(vmem(), vmem(), vmem()),
        compiler_params=params(),
        name="share",
    )(pieces)


def widen_kernel(own_ref, low_ref, high_ref, out_ref, *, parts):
    rows, width = own_ref.shape
    cols = width // LANE
    lane = lax.broadcasted_iota(jnp.int32, (rows, LANE), 1)
    patch = lax.axis_index("patch")
    low = low_ref[...].astype(f32) * (patch > 0).astype(f32)
    high = high_ref[...].astype(f32) * (patch < lax.axis_size("patch") - 1).astype(f32)
    before = pltpu.roll(low, PAD, 1)
    for c in range(cols + 1):
        here = own_ref[:, c * LANE : (c + 1) * LANE].astype(f32) if c < cols else high
        here = pltpu.roll(here, PAD, 1)
        block = jnp.where(lane < PAD, before, here).astype(bf16)
        for p in range(parts):
            out_ref[p, :, c * LANE : (c + 1) * LANE] = block
        before = here


def widen(own, low, high, parts):
    rows, width = own.shape
    return pl.pallas_call(
        functools.partial(widen_kernel, parts=parts),
        out_shape=jax.ShapeDtypeStruct((parts, rows, width + LANE), bf16),
        in_specs=[vmem()] * 3,
        out_specs=vmem(),
        compiler_params=params(),
        name="widen",
    )(own, low, high)


def match_kernel(
    count_ref,
    index_ref,
    slope_ref,
    wide_ref,
    vert_ref,
    horiz_ref,
    image_ref,
    template_ref,
    diff_ref,
    padded,
    vertical,
    held,
    arrived,
    sent,
    *,
    group,
):
    slots, rows, width = held.shape
    cols = width // LANE
    count = count_ref[0, 0]

    def fetch(s):
        return pltpu.make_async_copy(image_ref.at[s], held.at[s], arrived.at[s])

    def put(s):
        return pltpu.make_async_copy(held.at[s], diff_ref.at[s], sent.at[s])

    for s in range(slots):
        fetch(s).start()

    padded[0:PAD, :] = jnp.zeros((PAD, width + LANE), bf16)
    padded[PAD + rows :, :] = jnp.zeros((LANE - PAD, width + LANE), bf16)
    padded[PAD : PAD + rows, :] = wide_ref[...]

    profiles = vert_ref.shape[0]
    band = vert_ref[...].reshape(profiles * LANE, 2 * LANE)
    for n in range(rows // LANE):
        for j in range(0, cols + 1, 2):
            at = slice(j * LANE, min(j + 2, cols + 1) * LANE)
            part = jnp.dot(band, padded[n * LANE : (n + 2) * LANE, at], preferred_element_type=f32).astype(bf16)
            for b in range(profiles):
                vertical[b, n * LANE : (n + 1) * LANE, at] = part[b * LANE : (b + 1) * LANE]

    lane = lax.broadcasted_iota(jnp.int32, (LANE, LANE), 1)
    for n in range(rows // LANE):
        at = slice(n * LANE, (n + 1) * LANE)
        here = pltpu.roll(wide_ref[at, :LANE].astype(f32), LANE - PAD, 1)
        for c in range(cols):
            after = pltpu.roll(wide_ref[at, (c + 1) * LANE : (c + 2) * LANE].astype(f32), LANE - PAD, 1)
            template_ref[at, c * LANE : (c + 1) * LANE] = jnp.where(lane < LANE - PAD, here, after).astype(bf16)
            here = after

    start = lax.axis_index("patch") * width
    center = width * lax.axis_size("patch") / 2
    column = lax.broadcasted_iota(jnp.int32, (8, LANE), 1) + start

    def match_group(i, _):
        for g in range(group):
            fetch(i * group + g).wait()

        @pl.when(i * group < count)
        def _():
            for g in range(group):
                slot = i * group + g
                live = slot < count
                slope = slope_ref[0, slot]
                first, second, third = index_ref[slot, 0], index_ref[slot, 1], index_ref[slot, 2]
                bands = jnp.concatenate([horiz_ref[second], horiz_ref[third]], axis=1)
                for m in range(cols):
                    at = slice(m * LANE, (m + 1) * LANE)
                    position = ((column + m * LANE).astype(f32) + 0.5 - center) / center
                    factor = (slope * position)[0:1]
                    both = jnp.dot(vertical[first, :, m * LANE : (m + 2) * LANE], bands, preferred_element_type=f32)
                    matched = both[:, :LANE] + factor * both[:, LANE:]
                    result = jnp.where(live, held[slot, :, at].astype(f32) - matched, 0.0)
                    held[slot, :, at] = result.astype(bf16)

        @pl.when(i * group >= count)
        def _():
            for g in range(group):
                held[i * group + g] = jnp.zeros((rows, width), bf16)

        for g in range(group):
            put(i * group + g).start()
        return 0

    lax.fori_loop(0, slots // group, match_group, 0)
    for s in range(slots):
        put(s).wait()


def match(counts, index, slopes, wide, vert, horiz, images, group=GROUP):
    slots, rows, width = images.shape
    return pl.pallas_call(
        functools.partial(match_kernel, group=group),
        out_shape=(jax.ShapeDtypeStruct((rows, width), bf16), jax.ShapeDtypeStruct(images.shape, bf16)),
        in_specs=[smem()] * 3 + [vmem()] * 3 + [pl.BlockSpec(memory_space=pl.ANY)],
        out_specs=(vmem(), pl.BlockSpec(memory_space=pl.ANY)),
        scratch_shapes=[
            pltpu.VMEM((rows + LANE, width + LANE), bf16),
            pltpu.VMEM((vert.shape[0], rows, width + LANE), bf16),
            pltpu.VMEM(images.shape, bf16),
            pltpu.SemaphoreType.DMA((slots,)),
            pltpu.SemaphoreType.DMA((slots,)),
        ],
        compiler_params=params(),
        name="match",
    )(counts, index, slopes, wide, vert, horiz, images)


def on_device(images, counts, slot_weight, kernel_index, kernel_slope, tap_basis):
    slots, rows, width = images.shape
    parts = lax.axis_size("epoch")
    patches = lax.axis_size("patch")
    chunk = rows // parts
    partial = accumulate(counts, slot_weight, images, chunk)
    pieces = lax.all_to_all(partial, "epoch", 0, 0, tiled=True)
    own, first, last = share(pieces.reshape(parts, -1, LANE), chunk, width)
    ring = [(i, (i + 1) % patches) for i in range(patches)]
    low = lax.ppermute(last, "patch", ring)
    high = lax.ppermute(first, "patch", [(target, source) for source, target in ring])
    vert, horiz = tap_bands(tap_basis)
    copies = widen(own, low, high, parts)
    wide = lax.all_to_all(copies, "epoch", 0, 0, tiled=True).reshape(rows, width + LANE)
    template, differences = match(counts, kernel_index[0], kernel_slope, wide, vert, horiz, images)
    return (template, differences)


def solution(mesh):
    in_specs = (
        P("epoch", None, "patch"),
        P("patch", "epoch"),
        P("patch", "epoch"),
        P("patch", "epoch", None),
        P("patch", "epoch"),
        P(),
    )
    out_specs = (P(None, "patch"), P("epoch", None, "patch"))
    return jax.shard_map(
        on_device, mesh=mesh, in_specs=in_specs, out_specs=out_specs, check_vma=False
    )
```

time: 84.9 us -> 79.5 us (0.936)
  the two profiles are of different devices: /device:TPU:1 before, /device:TPU:9 now
where the time goes in v1:
time: 79.5 us; the launch traced here: 79.2 us
  blocking collectives  25.9 us (33%)
  Pallas kernels  22.1 us (28%)
  waiting for transfers between devices  19.7 us (25%)
  starting transfers between devices  9.53 us (12%)
  between operations  1.32 us (2%)
    all_to_all x1, blocking collectives, on_device(): pieces = lax.all_to_all(partial, 'epoch', 0, 0, tiled=True)  25.9 us
    all_to_all x1, waiting for transfers between devices, on_device(): lax.all_to_all(copies, 'epoch', 0, 0, tiled=True)  15.2 us
    pallas_call x1, Pallas kernels, match(): pl.pallas_call(functools.partial(match_kernel, group=group), out_shape=(j...  13.2 us
    pallas_call x1, Pallas kernels, accumulate(): pl.pallas_call(functools.partial(accumulate_kernel, chunk=chunk), out_sha...  5.62 us
    all_to_all x1, starting transfers between devices, on_device(): lax.all_to_all(copies, 'epoch', 0, 0, tiled=True)  4.9 us
    ppermute x1, starting transfers between devices, on_device(): low = lax.ppermute(last, 'patch', ring)  4.63 us
    ppermute x1, waiting for transfers between devices, on_device(): lax.ppermute(first, 'patch', [(target, source) for source, target in ring])  3.78 us
  transfers between devices with their start and end apart: 3, of which 3 were waited for; matrix products, arithmetic and copies ran while one was open for 0% of the time, Pallas kernels for 2%

profile of v1, /device:TPU:9, one launch (start us, length us, event | category | flops | bytes accessed | tf_op | source)
XLA Modules:
  0.0 79.2 jit_solution(16180702970317653335)
XLA Ops:
  1.3 0.0 copy-start.2
  1.3 0.6 copy-done.2
  1.9 5.6 %accumulate.1 = s32[2304,128]{1,0:T(8,128)S(1)} custom-call(s32[1,1]{1,0:T(1,128)S(6)} %copy.10.count_ref, f32[1,12]{1,0:T(1,128)S(1)} %copy-done.2, bf16[12,512,1024]{2,1,0:T(8,128)(2,1)} %image_ref.3), custom_call_target="tpu_custom_call" | custom-call | tf_op jit(solution)/shard_map/accumulate/pallas_call | solution.py:115
  7.6 25.9 %all_to_all.14.piece_ref = s32[32,72,128]{2,1,0:T(8,128)S(1)} all-to-all(s32[32,72,128]{2,1,0:T(8,128)S(1)} %bitcast.4), channel_id=1, replica_groups=mesh['patch'=4,'epoch'=32] {'epoch'}, dimensions={0} | all-to-all | bytes 2359296 | tf_op jit(solution)/shard_map/all_to_all | solution.py:314
  33.4 0.4 share.1
  33.8 4.6 %collective-permute-start = (bf16[16,128]{1,0:T(8,128)(2,1)S(1)}, bf16[16,128]{1,0:T(8,128)(2,1)S(1)}, u32[]{:S(2)}, u32[]{:S(2)}) collective-permute-start(bf16[16,128]{1,0:T(8,128)(2,1)S(1)} %get-tuple-element.8), channel_id=1, source_target_pairs={{0,32},{32,64},{64,96},{96,0},{1,33},{33,65},{65,97},{97,1},{2,34}... | collective-permute-start | bytes 12296 | tf_op jit(solution)/shard_map/ppermute | solution.py:317
  38.5 0.0 collective-permute-start.1
  38.5 0.8 collective-permute-done.low_ref
  39.2 3.8 %collective-permute-done.1.high_ref = bf16[16,128]{1,0:T(8,128)(2,1)S(1)} collective-permute-done((bf16[16,128]{1,0:T(8,128)(2,1)S(1)}, bf16[16,128]{1,0:T(8,128)(2,1)S(1)}, u32[]{:S(2)}, u32[]{:S(2)}) %collective-permute-start.1) | collective-permute-done | bytes 4128 | tf_op jit(solution)/shard_map/ppermute | solution.py:318
  43.0 1.2 %widen.1 = bf16[32,16,1152]{2,1,0:T(8,128)(2,1)} custom-call(bf16[16,1024]{1,0:T(8,128)(2,1)S(1)} %get-tuple-element.7.own_ref, bf16[16,128]{1,0:T(8,128)(2,1)S(1)} %collective-permute-done.low_ref, bf16[16,128]{1,0:T(8,128)(2,1)S(1)} %collective-permute-done.1.high_ref), custom_call_target="tpu_custom_call" | custom-call | tf_op jit(solution)/shard_map/widen/pallas_call | solution.py:187
  44.2 0.0 copy-start.3
  44.2 0.0 copy-start
  44.2 0.0 copy-start.1
  44.2 4.9 %all-to-all-start.1 = ((bf16[32,16,1152]{2,1,0:T(8,128)(2,1)}), bf16[32,16,1152]{2,1,0:T(8,128)(2,1)S(1)}, u32[]{:S(2)}, u32[]{:S(2)}) async-start(bf16[32,16,1152]{2,1,0:T(8,128)(2,1)} %widen.1), calls=%async_computation.1 | async-start | bytes 2359296 | tf_op jit(solution)/shard_map/all_to_all | solution.py:321
  49.1 0.0 copy-done.3
  49.2 0.1 copy.9
  49.3 0.0 copy-done
  49.3 1.6 %tap_bands.1 = (bf16[8,128,256]{2,1,0:T(8,128)(2,1)S(1)}, bf16[8,256,128]{2,1,0:T(8,128)(2,1)S(1)}) custom-call(f32[8,21]{1,0:T(8,128)S(1)} %copy-done), custom_call_target="tpu_custom_call" | custom-call | tf_op jit(solution)/shard_map/tap_bands/pallas_call | solution.py:56
  50.8 15.2 %all-to-all-done.1 = bf16[32,16,1152]{2,1,0:T(8,128)(2,1)S(1)} async-done(((bf16[32,16,1152]{2,1,0:T(8,128)(2,1)}), bf16[32,16,1152]{2,1,0:T(8,128)(2,1)S(1)}, u32[]{:S(2)}, u32[]{:S(2)}) %all-to-all-start.1) | async-done | bytes 1179680 | tf_op jit(solution)/shard_map/all_to_all | solution.py:321
  66.0 0.0 copy-done.1
  66.0 13.2 %match.1 = (bf16[512,1024]{1,0:T(8,128)(2,1)}, bf16[12,512,1024]{2,1,0:T(8,128)(2,1)}) custom-call(s32[1,1]{1,0:T(1,128)S(6)} %copy.10.count_ref, s32[12,3]{1,0:T(8,128)S(1)} %bitcast.5, f32[1,12]{1,0:T(1,128)S(1)} %copy-done.1, bf16[512,1152]{1,0:T(8,128)(2,1)S(1)} %bitcast.3, bf16[8,128,256]{2,1,0:T(8,128)(2,1)S(1)} %get-tuple-element.10.vert_ref, ...), custom_call_target="tpu_custom_call" | custom-call | tf_op jit(solution)/shard_map/match/pallas_call | solution.py:291
Async XLA Ops:
  1.3 0.7 copy-start.2
  33.8 5.4 %collective-permute-start = (bf16[16,128]{1,0:T(8,128)(2,1)S(1)}, bf16[16,128]{1,0:T(8,128)(2,1)S(1)}, u32[]{:S(2)}, u32[]{:S(2)}) collective-permute-start(bf16[16,128]{1,0:T(8,128)(2,1)S(1)} %get-tuple-element.8), channel_id=1, source_target_pairs={{0,32},{32,64},{64,96},{96,0},{1,33},{33,65},{65,97},{97,1},{2,34}... | collective-permute-start | bytes 12296 | tf_op jit(solution)/shard_map/ppermute | solution.py:317
  38.5 4.5 %collective-permute-start.1 = (bf16[16,128]{1,0:T(8,128)(2,1)S(1)}, bf16[16,128]{1,0:T(8,128)(2,1)S(1)}, u32[]{:S(2)}, u32[]{:S(2)}) collective-permute-start(bf16[16,128]{1,0:T(8,128)(2,1)S(1)} %get-tuple-element.9), channel_id=1, source_target_pairs={{32,0},{64,32},{96,64},{0,96},{33,1},{65,33},{97,65},{1,97},{34,2}... | collective-permute-start | bytes 12296 | tf_op jit(solution)/shard_map/ppermute | solution.py:318
  44.2 4.9 %copy-start.3 = (s32[1,12,3]{1,0,2:T(1,128)S(1)}, s32[1,12,3]{1,0,2:T(1,128)}, u32[]{:S(2)}) copy-start(s32[1,12,3]{1,0,2:T(1,128)} %param.9) | copy-start | bytes 436
  44.2 5.0 %copy-start = (f32[8,21]{1,0:T(8,128)S(1)}, f32[8,21]{1,0:T(8,128)}, u32[]{:S(2)}) copy-start(f32[8,21]{1,0:T(8,128)} %basis_ref.1) | copy-start | bytes 2020
  44.2 21.8 %copy-start.1 = (f32[1,12]{1,0:T(1,128)S(1)}, f32[1,12]{1,0:T(1,128)}, u32[]{:S(2)}) copy-start(f32[1,12]{1,0:T(1,128)} %slope_ref.1) | copy-start | bytes 148
  44.2 21.8 %all-to-all-start.1 = ((bf16[32,16,1152]{2,1,0:T(8,128)(2,1)}), bf16[32,16,1152]{2,1,0:T(8,128)(2,1)S(1)}, u32[]{:S(2)}, u32[]{:S(2)}) async-start(bf16[32,16,1152]{2,1,0:T(8,128)(2,1)} %widen.1), calls=%async_computation.1 | async-start | bytes 2359296 | tf_op jit(solution)/shard_map/all_to_all | solution.py:321

commit v2 on v1

v2 whole, which is shorter than its diff:
```python
import functools

import jax
import jax.numpy as jnp
from jax import lax
from jax.experimental import pallas as pl
from jax.experimental.pallas import tpu as pltpu
from jax.sharding import PartitionSpec as P

f32 = jnp.float32
bf16 = jnp.bfloat16
LANE = 128
STEPS = 32767.0
WEIGHT_STEPS = 2.0**17
PAD = 16
GROUP = 2


def smem():
    return pl.BlockSpec(memory_space=pltpu.SMEM)


def vmem():
    return pl.BlockSpec(memory_space=pltpu.VMEM)


def params(limit):
    return pltpu.CompilerParams(vmem_limit_bytes=limit * 2**20)


def bands_kernel(basis_ref, image_ref, vert_ref, horiz_ref, held_ref, arrived):
    fetches = [
        pltpu.make_async_copy(image_ref.at[s], held_ref.at[s], arrived.at[s]) for s in range(image_ref.shape[0])
    ]
    for copy in fetches:
        copy.start()
    profiles, taps = basis_ref.shape
    lead = PAD - taps // 2
    lane = lax.broadcasted_iota(jnp.int32, (8, 2 * LANE), 1)

    def body(b, _):
        down = jnp.zeros((8, 2 * LANE), f32)
        across = jnp.zeros((8, 2 * LANE), f32)
        for t in range(taps):
            down = jnp.where(lane == lead + t, basis_ref[b, t], down)
            across = jnp.where(lane == 2 * LANE - lead - t, basis_ref[b, t], across)
        for base in range(0, 2 * LANE, 16):
            if base < LANE:
                halves = [pltpu.roll(down, base + 8 * h, 1, stride=1, stride_axis=0) for h in range(2)]
                vert_ref[b, base : base + 16, :] = jnp.concatenate(halves, axis=0).astype(bf16)
            halves = [pltpu.roll(across, base + 8 * h, 1, stride=1, stride_axis=0) for h in range(2)]
            horiz_ref[b, base : base + 16, :] = jnp.concatenate(halves, axis=0)[:, :LANE].astype(bf16)
        return 0

    lax.fori_loop(0, profiles, body, 0)
    for copy in fetches:
        copy.wait()


def tap_bands(basis, images):
    profiles = basis.shape[0]
    return pl.pallas_call(
        bands_kernel,
        out_shape=(
            jax.ShapeDtypeStruct((profiles, LANE, 2 * LANE), bf16),
            jax.ShapeDtypeStruct((profiles, 2 * LANE, LANE), bf16),
            jax.ShapeDtypeStruct(images.shape, bf16),
        ),
        in_specs=[smem(), pl.BlockSpec(memory_space=pl.ANY)],
        out_specs=(vmem(), vmem(), vmem()),
        scratch_shapes=[pltpu.SemaphoreType.DMA((images.shape[0],))],
        compiler_params=params(38),
        name="tap_bands",
    )(basis, images)


def pack(parts, weight_word, out_ref, base):
    top = jnp.abs(parts[0])
    for part in parts[1:]:
        top = jnp.maximum(top, jnp.abs(part))
    exponent = jnp.ceil(jnp.log2(jnp.maximum(top, 1e-30)) + 0.002)
    factor = STEPS / jnp.exp2(exponent)
    words = [jnp.round(part * factor).astype(jnp.int32) for part in parts]
    half = len(parts) // 2
    for i in range(half):
        out_ref[base + 8 * i : base + 8 * i + 8, :] = (words[half + i] << 16) | (words[i] & 0xFFFF)
    out_ref[base + 8 * half : base + 8 * half + 8, :] = weight_word + (exponent.astype(jnp.int32) + 128)


def accumulate_kernel(counts_ref, weights_ref, image_ref, out_ref, held, arrived, count_ref, weight_ref, placed, *, chunk):
    slots, rows, width = image_ref.shape
    blocks, _, block, _ = held.shape
    copies = [
        pltpu.make_async_copy(image_ref.at[:, n * block : (n + 1) * block, :], held.at[n], arrived.at[n])
        for n in range(blocks)
    ]
    small = (
        pltpu.make_async_copy(counts_ref, count_ref, placed.at[0]),
        pltpu.make_async_copy(weights_ref, weight_ref, placed.at[1]),
    )
    for copy in (*small, *copies):
        copy.start()
    for copy in small:
        copy.wait()
    weights = [jnp.where(s < count_ref[0, 0], weight_ref[0, s], 0.0) for s in range(slots)]
    total = weights[0]
    for s in range(1, slots):
        total = total + weights[s]
    weight_word = jnp.round(jnp.full((8, LANE), total, f32) * WEIGHT_STEPS).astype(jnp.int32) << 8
    cols = width // LANE
    stride = (cols + 1) * 8
    for n, copy in enumerate(copies):
        copy.wait()
        for q in range(block // chunk):
            upper, lower = [], []
            for c in range(cols):
                at = slice(c * LANE, (c + 1) * LANE)
                here = slice(q * chunk, (q + 1) * chunk)
                part = held[n, 0, here, at].astype(f32) * weights[0]
                for s in range(1, slots):
                    part = part + held[n, s, here, at].astype(f32) * weights[s]
                upper.append(part[:8])
                lower.append(part[8:])
            pack(upper + lower, weight_word, out_ref, (n * (block // chunk) + q) * stride)


def accumulate(counts, weight, images, chunk=16, block=64):
    slots, rows, width = images.shape
    return pl.pallas_call(
        functools.partial(accumulate_kernel, chunk=chunk),
        out_shape=jax.ShapeDtypeStruct((rows // chunk * (width // LANE + 1) * 8, LANE), jnp.int32),
        in_specs=[pl.BlockSpec(memory_space=pl.ANY)] * 3,
        out_specs=vmem(),
        scratch_shapes=[
            pltpu.VMEM((rows // block, slots, block, width), bf16),
            pltpu.SemaphoreType.DMA((rows // block,)),
            pltpu.SMEM(counts.shape, jnp.int32),
            pltpu.SMEM(weight.shape, f32),
            pltpu.SemaphoreType.DMA((2,)),
        ],
        compiler_params=params(50),
        name="accumulate",
    )(counts, weight, images)


def share_kernel(piece_ref, out_ref):
    parts, chunk, width = out_ref.shape
    cols = width // LANE
    upper, lower, weight = [None] * cols, [None] * cols, None
    for p in range(parts):
        meta = piece_ref[p, 8 * cols :, :]
        weight = meta >> 8 if weight is None else weight + (meta >> 8)
        scale = jnp.exp2(((meta & 0xFF) - 128).astype(f32)) / STEPS
        for c in range(cols):
            word = piece_ref[p, 8 * c : 8 * c + 8, :]
            up = ((word << 16) >> 16).astype(f32) * scale
            low = (word >> 16).astype(f32) * scale
            upper[c] = up if p == 0 else upper[c] + up
            lower[c] = low if p == 0 else lower[c] + low
    weight = weight.astype(f32) / WEIGHT_STEPS
    lane = lax.broadcasted_iota(jnp.int32, (chunk, LANE), 1)
    turned = [
        pltpu.roll(jnp.concatenate([upper[c] / weight, lower[c] / weight], axis=0), PAD, 1) for c in range(cols)
    ]
    for c in range(cols):
        block = jnp.where(lane < PAD, turned[c - 1], turned[c]).astype(bf16)
        for p in range(parts):
            out_ref[p, :, c * LANE : (c + 1) * LANE] = block


def share(pieces, chunk, width):
    parts = pieces.shape[0]
    return pl.pallas_call(
        share_kernel,
        out_shape=jax.ShapeDtypeStruct((parts, chunk, width), bf16),
        in_specs=[vmem()],
        out_specs=vmem(),
        compiler_params=params(16),
        name="share",
    )(pieces)


def vertical_step(vert_ref, padded, store):
    profiles = vert_ref.shape[0]
    rows, width = padded.shape[0] - LANE, padded.shape[1]
    band = vert_ref[...].reshape(profiles * LANE, 2 * LANE)
    for n in range(rows // LANE):
        for j in range(0, width, 2 * LANE):
            at = slice(j, min(j + 2 * LANE, width))
            part = jnp.dot(band, padded[n * LANE : (n + 2) * LANE, at], preferred_element_type=f32).astype(bf16)
            for b in range(profiles):
                store(b, slice(n * LANE, (n + 1) * LANE), at, part[b * LANE : (b + 1) * LANE])


def pack_ends_kernel(turned_ref, out_ref):
    part = out_ref.shape[0]
    lane = lax.broadcasted_iota(jnp.int32, out_ref.shape, 1)
    ends = turned_ref[:part, :LANE].astype(f32)
    for n in range(1, turned_ref.shape[0] // part):
        here = pltpu.roll(turned_ref[n * part : (n + 1) * part, :LANE].astype(f32), 2 * PAD * n, 1)
        ends = jnp.where(lane < 2 * PAD * n, ends, here)
    out_ref[...] = ends.astype(bf16)


def pack_ends(turned):
    return pl.pallas_call(
        pack_ends_kernel,
        out_shape=jax.ShapeDtypeStruct((turned.shape[0] * 2 * PAD // LANE, LANE), bf16),
        grid=(1,),
        in_specs=[pl.BlockSpec((turned.shape[0], LANE), lambda i: (0, 0))],
        out_specs=pl.BlockSpec((turned.shape[0] * 2 * PAD // LANE, LANE), lambda i: (0, 0)),
        compiler_params=params(16),
        name="pack_ends",
    )(turned)


def inner_kernel(turned_ref, vert_ref, template_ref, vertical_ref, padded, template, written):
    rows, width = turned_ref.shape
    cols = width // LANE
    padded[0:PAD, :] = jnp.zeros((PAD, width - LANE), bf16)
    padded[PAD + rows :, :] = jnp.zeros((LANE - PAD, width - LANE), bf16)
    padded[PAD : PAD + rows, :] = turned_ref[:, LANE:]

    lane = lax.broadcasted_iota(jnp.int32, (LANE, LANE), 1)
    for n in range(rows // LANE):
        at = slice(n * LANE, (n + 1) * LANE)
        back = [
            pltpu.roll(turned_ref[at, c * LANE : (c + 1) * LANE].astype(f32), LANE - PAD, 1) for c in range(cols)
        ]
        for c in range(cols):
            block = jnp.where(lane < LANE - PAD, back[c], back[(c + 1) % cols])
            template[at, c * LANE : (c + 1) * LANE] = block.astype(bf16)
    copy = pltpu.make_async_copy(template, template_ref, written)
    copy.start()

    def store(b, at, to, part):
        vertical_ref[b, at, to] = part

    @pl.loop(0, 1)
    def _(_):
        vertical_step(vert_ref, padded, store)

    copy.wait()


def match_inner(turned, vert):
    rows, width = turned.shape
    hbm = pl.BlockSpec(memory_space=pl.ANY)
    return pl.pallas_call(
        inner_kernel,
        out_shape=(
            jax.ShapeDtypeStruct((rows, width), bf16),
            jax.ShapeDtypeStruct((vert.shape[0], rows, width - LANE), bf16),
        ),
        in_specs=[vmem(), vmem()],
        out_specs=(hbm, vmem()),
        scratch_shapes=[
            pltpu.VMEM((rows + LANE, width - LANE), bf16),
            pltpu.VMEM((rows, width), bf16),
            pltpu.SemaphoreType.DMA,
        ],
        cost_estimate=pl.CostEstimate(flops=10**10, bytes_accessed=10**7, transcendentals=0),
        compiler_params=params(16),
        name="match_inner",
    )(turned, vert)


def match_kernel(
    count_ref,
    index_ref,
    slope_ref,
    turned_ref,
    low_ref,
    high_ref,
    vert_ref,
    horiz_ref,
    inner_ref,
    image_ref,
    diff_ref,
    padded,
    outer,
    staged,
    sent,
    *,
    group,
):
    slots, rows, width = staged.shape
    cols = width // LANE
    count = count_ref[0, 0]
    patch = lax.axis_index("patch")

    def put(s):
        return pltpu.make_async_copy(staged.at[s], diff_ref.at[s], sent.at[s])

    @pl.when(count > 0)
    def _():
        padded[0:PAD, :] = jnp.zeros((PAD, 2 * LANE), bf16)
        padded[PAD + rows :, :] = jnp.zeros((LANE - PAD, 2 * LANE), bf16)
        part = low_ref.shape[0]
        lane = lax.broadcasted_iota(jnp.int32, (part, LANE), 1)
        low = low_ref[...].astype(f32) * (patch > 0).astype(f32)
        high = high_ref[...].astype(f32) * (patch < lax.axis_size("patch") - 1).astype(f32)
        for n in range(rows // part):
            own = turned_ref[n * part : (n + 1) * part, :LANE].astype(f32)
            left = pltpu.roll(low, LANE - 2 * PAD * n, 1) if n else low
            right = pltpu.roll(high, LANE - 2 * PAD * n, 1) if n else high
            at = slice(PAD + n * part, PAD + (n + 1) * part)
            padded[at, :LANE] = jnp.where(lane < PAD, left, own).astype(bf16)
            padded[at, LANE:] = jnp.where(lane < PAD, own, right).astype(bf16)

        def store(b, at, _, part):
            outer[b, at, :LANE] = part[:, :LANE]
            outer[b, at, 3 * LANE :] = part[:, LANE:]

        vertical_step(vert_ref, padded, store)
        for b in range(vert_ref.shape[0]):
            outer[b, :, LANE : 2 * LANE] = inner_ref[b, :, :LANE]
            outer[b, :, 2 * LANE : 3 * LANE] = inner_ref[b, :, width - 2 * LANE :]

    center = width * lax.axis_size("patch") / 2
    column = lax.broadcasted_iota(jnp.int32, (8, LANE), 1) + patch * width

    def match_group(i, _):
        @pl.when(i * group < count)
        def _():
            for g in range(group):
                slot = i * group + g
                live = slot < count
                slope = slope_ref[0, slot]
                first, second, third = index_ref[slot, 0], index_ref[slot, 1], index_ref[slot, 2]
                bands = jnp.concatenate([horiz_ref[second], horiz_ref[third]], axis=1)
                for m in range(cols):
                    at = slice(m * LANE, (m + 1) * LANE)
                    if m == 0:
                        window = outer[first, :, : 2 * LANE]
                    elif m == cols - 1:
                        window = outer[first, :, 2 * LANE :]
                    else:
                        window = inner_ref[first, :, (m - 1) * LANE : (m + 1) * LANE]
                    position = ((column + m * LANE).astype(f32) + 0.5 - center) / center
                    factor = (slope * position)[0:1]
                    both = jnp.dot(window, bands, preferred_element_type=f32)
                    matched = both[:, :LANE] + factor * both[:, LANE:]
                    result = jnp.where(live, image_ref[slot, :, at].astype(f32) - matched, 0.0)
                    staged[slot, :, at] = result.astype(bf16)
                put(slot).start()

        @pl.when(i * group >= count)
        def _():
            for g in range(group):
                staged[i * group + g] = jnp.zeros((rows, width), bf16)
                put(i * group + g).start()

        return 0

    lax.fori_loop(0, slots // group, match_group, 0)
    for s in range(slots):
        put(s).wait()


def match(counts, index, slopes, turned, low, high, vert, horiz, inner, images, group=GROUP):
    slots, rows, width = images.shape
    return pl.pallas_call(
        functools.partial(match_kernel, group=group),
        out_shape=jax.ShapeDtypeStruct(images.shape, bf16),
        in_specs=[smem()] * 3 + [vmem()] * 7,
        out_specs=pl.BlockSpec(memory_space=pl.ANY),
        scratch_shapes=[
            pltpu.VMEM((rows + LANE, 2 * LANE), bf16),
            pltpu.VMEM((vert.shape[0], rows, 4 * LANE), bf16),
            pltpu.VMEM(images.shape, bf16),
            pltpu.SemaphoreType.DMA((slots,)),
        ],
        compiler_params=params(24),
        name="match",
    )(counts, index, slopes, turned, low, high, vert, horiz, inner, images)


def on_device(images, counts, slot_weight, kernel_index, kernel_slope, tap_basis):
    slots, rows, width = images.shape
    parts = lax.axis_size("epoch")
    patches = lax.axis_size("patch")
    chunk = rows // parts
    partial = accumulate(counts, slot_weight, images, chunk)
    pieces = lax.all_to_all(partial, "epoch", 0, 0, tiled=True)
    copies = share(pieces.reshape(parts, -1, LANE), chunk, width)
    turned = lax.all_to_all(copies, "epoch", 0, 0, tiled=True).reshape(rows, width)
    vert, horiz, held = tap_bands(tap_basis, images)
    ring = [(i, (i + 1) % patches) for i in range(patches)]
    ends = pack_ends(turned)
    low = lax.ppermute(ends, "patch", ring)
    high = lax.ppermute(ends, "patch", [(target, source) for source, target in ring])
    template, inner = match_inner(turned, vert)
    differences = match(
        counts, kernel_index[0], kernel_slope, turned, low, high, vert, horiz, inner, held
    )
    return (template, differences)


def solution(mesh):
    in_specs = (
        P("epoch", None, "patch"),
        P("patch", "epoch"),
        P("patch", "epoch"),
        P("patch", "epoch", None),
        P("patch", "epoch"),
        P(),
    )
    out_specs = (P(None, "patch"), P("epoch", None, "patch"))
    return jax.shard_map(
        on_device, mesh=mesh, in_specs=in_specs, out_specs=out_specs, check_vma=False
    )
```

time: 79.5 us -> 74.7 us (0.940)
  waiting for transfers between devices: 19.7 us -> 6.21 us
  local copies, waits for them, and re-layouts: 0.75 us -> 5.54 us
  Pallas kernels: 22.1 us -> 24.1 us
  starting transfers between devices: 9.53 us -> 10.7 us
    all_to_all x1, waiting for transfers between devices: 15.2 us -> 4.73 us  [on_device(): lax.all_to_all(copies, 'epoch', 0, 0, tiled=True).reshape(rows, width)]
    unnamed x8 -> x16, local copies, waits for them, and re-layouts: 0.66 us -> 5.45 us
    pallas_call x1, Pallas kernels: 1.55 us -> 5.3 us  [tap_bands(): pl.pallas_call(bands_kernel, out_shape=(jax.ShapeDtypeStruct((profiles, L...]
    ppermute x2, waiting for transfers between devices: 4.53 us -> 1.47 us  [the longest x1 1.47 us: on_device(): lax.ppermute(ends, 'patch', [(target, source) for source, target in ring])]
    pallas_call x3 -> x4, Pallas kernels: 14.9 us -> 13.7 us  [the longest x1 8.58 us: match(): pl.pallas_call(functools.partial(match_kernel, group=group), out_shape=ja...]
  transfers between devices with their start and end apart: 3 -> 3, of which waited for: 3 -> 2; matrix products, arithmetic and copies ran while one was open for 0% -> 0% of each run, Pallas kernels for 2% -> 12%
where the time goes in v2:
time: 74.7 us; the launch traced here: 73.7 us
  blocking collectives  25.9 us (35%)
  Pallas kernels  24.1 us (32%)
  starting transfers between devices  10.7 us (14%)
  waiting for transfers between devices  6.21 us (8%)
  local copies, waits for them, and re-layouts  5.54 us (7%)
  between operations  1.41 us (2%)
    all_to_all x1, blocking collectives, on_device(): pieces = lax.all_to_all(partial, 'epoch', 0, 0, tiled=True)  25.9 us
    pallas_call x1, Pallas kernels, match(): pl.pallas_call(functools.partial(match_kernel, group=group), out_shape=ja...  8.58 us
    all_to_all x1, starting transfers between devices, on_device(): lax.all_to_all(copies, 'epoch', 0, 0, tiled=True).reshape(rows, width)  5.48 us
    unnamed x16, local copies, waits for them, and re-layouts  5.45 us
    pallas_call x1, Pallas kernels, tap_bands(): pl.pallas_call(bands_kernel, out_shape=(jax.ShapeDtypeStruct((profiles, L...  5.3 us
    ppermute x1, starting transfers between devices, on_device(): low = lax.ppermute(ends, 'patch', ring)  5.2 us
    pallas_call x1, Pallas kernels, accumulate(): pl.pallas_call(functools.partial(accumulate_kernel, chunk=chunk), out_sha...  5.1 us
    all_to_all x1, waiting for transfers between devices, on_device(): lax.all_to_all(copies, 'epoch', 0, 0, tiled=True).reshape(rows, width)  4.73 us
  transfers between devices with their start and end apart: 3, of which 2 were waited for; matrix products, arithmetic and copies ran while one was open for 0% of the time, Pallas kernels for 12%

profile of v2, /device:TPU:9, one launch (start us, length us, event | category | flops | bytes accessed | tf_op | source)
XLA Modules:
  0.0 73.7 jit_solution(17760841398259739430)
XLA Ops:
  0.6 0.0 copy-start.1
  1.3 0.0 copy-start.2
  1.3 0.6 copy-done.2
  2.0 5.1 %accumulate.1 = s32[2304,128]{1,0:T(8,128)S(1)} custom-call(s32[1,1]{1,0:T(1,128)S(6)} %copy.10.counts_ref.count_ref, f32[1,12]{1,0:T(1,128)S(1)} %copy-done.2, bf16[12,512,1024]{2,1,0:T(8,128)(2,1)} %image_ref.3), custom_call_target="tpu_custom_call" | custom-call | tf_op jit(solution)/shard_map/accumulate/pallas_call | solution.py:129
  7.1 0.0 copy-start.4
  7.1 25.9 %all_to_all.14.piece_ref = s32[32,72,128]{2,1,0:T(8,128)S(1)} all-to-all(s32[32,72,128]{2,1,0:T(8,128)S(1)} %bitcast.8), channel_id=1, replica_groups=mesh['patch'=4,'epoch'=32] {'epoch'}, dimensions={0} | all-to-all | bytes 2359296 | tf_op jit(solution)/shard_map/all_to_all | solution.py:385
  32.9 1.6 %share.1 = bf16[32,16,1024]{2,1,0:T(8,128)(2,1)} custom-call(s32[32,72,128]{2,1,0:T(8,128)S(1)} %all_to_all.14.piece_ref), custom_call_target="tpu_custom_call" | custom-call | tf_op jit(solution)/shard_map/share/pallas_call | solution.py:173
  34.5 5.5 %all-to-all-start.1 = ((bf16[32,16,1024]{2,1,0:T(8,128)(2,1)}), bf16[32,16,1024]{2,1,0:T(8,128)(2,1)S(1)}, u32[]{:S(2)}, u32[]{:S(2)}) async-start(bf16[32,16,1024]{2,1,0:T(8,128)(2,1)} %share.1), calls=%async_computation.1 | async-start | bytes 2097152 | tf_op jit(solution)/shard_map/all_to_all | solution.py:387
  40.0 0.0 copy-done.1
  40.0 5.3 %tap_bands.1 = (bf16[8,128,256]{2,1,0:T(8,128)(2,1)S(1)}, bf16[8,256,128]{2,1,0:T(8,128)(2,1)S(1)}, bf16[12,512,1024]{2,1,0:T(8,128)(2,1)S(1)}) custom-call(f32[8,21]{1,0:T(8,128)S(1)} %copy-done.1, bf16[12,512,1024]{2,1,0:T(8,128)(2,1)} %image_ref.3), custom_call_target="tpu_custom_call" | custom-call | tf_op jit(solution)/shard_map/tap_bands/pallas_call | solution.py:62
  45.3 0.0 copy-start
  45.4 4.8 %copy-done = bf16[12,512,1024]{2,1,0:T(8,128)(2,1)} copy-done((bf16[12,512,1024]{2,1,0:T(8,128)(2,1)}, bf16[12,512,1024]{2,1,0:T(8,128)(2,1)S(1)}, u32[]{:S(2)}) %copy-start) | copy-done | bytes 12582936
  50.1 0.0 copy-done.4
  50.1 0.1 copy.9
  50.2 4.7 %all-to-all-done.1 = bf16[32,16,1024]{2,1,0:T(8,128)(2,1)S(1)} async-done(((bf16[32,16,1024]{2,1,0:T(8,128)(2,1)}), bf16[32,16,1024]{2,1,0:T(8,128)(2,1)S(1)}, u32[]{:S(2)}, u32[]{:S(2)}) %all-to-all-start.1) | async-done | bytes 1048608 | tf_op jit(solution)/shard_map/all_to_all | solution.py:387
  55.0 0.1 pack_ends.1
  55.1 5.2 %collective-permute-start = (bf16[128,128]{1,0:T(8,128)(2,1)S(1)}, bf16[128,128]{1,0:T(8,128)(2,1)S(1)}, u32[]{:S(2)}, u32[]{:S(2)}) collective-permute-start(bf16[128,128]{1,0:T(8,128)(2,1)S(1)} %pack_ends.1), channel_id=1, source_target_pairs={{0,32},{32,64},{64,96},{96,0},{1,33},{33,65},{65,97},{97,1},{2,34}... | collective-permute-start | bytes 98312 | tf_op jit(solution)/shard_map/ppermute | solution.py:391
  60.3 0.0 collective-permute-start.1
  60.3 3.3 %match_inner.1 = (bf16[512,1024]{1,0:T(8,128)(2,1)}, bf16[8,512,896]{2,1,0:T(8,128)(2,1)S(1)}) custom-call(bf16[512,1024]{1,0:T(8,128)(2,1)S(1)} %bitcast.6, bf16[8,128,256]{2,1,0:T(8,128)(2,1)S(1)} %get-tuple-element.7.vert_ref), custom_call_target="tpu_custom_call" | custom-call | flops 10000000000 | bytes 10000000 | tf_op jit(solution)/shard_map/match_inner/pallas_call | solution.py:249
  63.7 0.0 collective-permute-done.low_ref
  63.7 1.5 %collective-permute-done.1.high_ref = bf16[128,128]{1,0:T(8,128)(2,1)S(1)} collective-permute-done((bf16[128,128]{1,0:T(8,128)(2,1)S(1)}, bf16[128,128]{1,0:T(8,128)(2,1)S(1)}, u32[]{:S(2)}, u32[]{:S(2)}) %collective-permute-start.1) | collective-permute-done | bytes 32800 | tf_op jit(solution)/shard_map/ppermute | solution.py:392
  65.1 0.0 slice-done
  65.1 0.0 slice-done.1
  65.2 8.6 %match.1 = bf16[12,512,1024]{2,1,0:T(8,128)(2,1)} custom-call(s32[1,1]{1,0:T(1,128)S(6)} %copy.10.counts_ref.count_ref, s32[12,3]{1,0:T(8,128)S(1)} %bitcast.9, f32[1,12]{1,0:T(1,128)S(1)} %copy-done.3, bf16[512,1024]{1,0:T(8,128)(2,1)S(1)} %bitcast.7, bf16[128,128]{1,0:T(8,128)(2,1)S(1)} %collective-permute-done.low_ref, ...), custom_call_target="tpu_custom_call" | custom-call | tf_op jit(solution)/shard_map/match/pallas_call | solution.py:363
  (7 shorter events, 0.0 us)
Async XLA Ops:
  0.6 39.4 %copy-start.1 = (f32[8,21]{1,0:T(8,128)S(1)}, f32[8,21]{1,0:T(8,128)}, u32[]{:S(2)}) copy-start(f32[8,21]{1,0:T(8,128)} %basis_ref.1) | copy-start | bytes 2020
  1.3 0.7 copy-start.2
  7.1 43.1 %copy-start.4 = (s32[1,12,3]{1,0,2:T(1,128)S(1)}, s32[1,12,3]{1,0,2:T(1,128)}, u32[]{:S(2)}) copy-start(s32[1,12,3]{1,0,2:T(1,128)} %param.9) | copy-start | bytes 436
  34.5 20.4 %all-to-all-start.1 = ((bf16[32,16,1024]{2,1,0:T(8,128)(2,1)}), bf16[32,16,1024]{2,1,0:T(8,128)(2,1)S(1)}, u32[]{:S(2)}, u32[]{:S(2)}) async-start(bf16[32,16,1024]{2,1,0:T(8,128)(2,1)} %share.1), calls=%async_computation.1 | async-start | bytes 2097152 | tf_op jit(solution)/shard_map/all_to_all | solution.py:387
  45.3 4.8 %copy-start = (bf16[12,512,1024]{2,1,0:T(8,128)(2,1)}, bf16[12,512,1024]{2,1,0:T(8,128)(2,1)S(1)}, u32[]{:S(2)}) copy-start(bf16[12,512,1024]{2,1,0:T(8,128)(2,1)S(1)} %get-tuple-element.11.image_ref) | copy-start | bytes 37748740
  55.0 10.2 %slice-start = ((s8[12582912]{0:T(1024)(128)(4,1)}), s8[4194304]{0:T(1024)(128)(4,1)S(1)}, s32[]{:S(2)}) async-start(s8[12582912]{0:T(1024)(128)(4,1)} %bitcast.3), calls=%async_computation.2 | async-start | bytes 8388608
  55.1 8.6 %collective-permute-start = (bf16[128,128]{1,0:T(8,128)(2,1)S(1)}, bf16[128,128]{1,0:T(8,128)(2,1)S(1)}, u32[]{:S(2)}, u32[]{:S(2)}) collective-permute-start(bf16[128,128]{1,0:T(8,128)(2,1)S(1)} %pack_ends.1), channel_id=1, source_target_pairs={{0,32},{32,64},{64,96},{96,0},{1,33},{33,65},{65,97},{97,1},{2,34}... | collective-permute-start | bytes 98312 | tf_op jit(solution)/shard_map/ppermute | solution.py:391
  60.3 4.8 %collective-permute-start.1 = (bf16[128,128]{1,0:T(8,128)(2,1)S(1)}, bf16[128,128]{1,0:T(8,128)(2,1)S(1)}, u32[]{:S(2)}, u32[]{:S(2)}) collective-permute-start(bf16[128,128]{1,0:T(8,128)(2,1)S(1)} %pack_ends.1), channel_id=1, source_target_pairs={{32,0},{64,32},{96,64},{0,96},{33,1},{65,33},{97,65},{1,97},{34,2}... | collective-permute-start | bytes 98312 | tf_op jit(solution)/shard_map/ppermute | solution.py:392
  60.3 4.8 %slice-start.1 = ((s8[12582912]{0:T(1024)(128)(4,1)}), s8[4194304]{0:T(1024)(128)(4,1)S(1)}, s32[]{:S(2)}) async-start(s8[12582912]{0:T(1024)(128)(4,1)} %bitcast.3), calls=%async_computation.3 | async-start | bytes 8388608
  60.3 4.8 %slice-start.2 = ((s8[12582912]{0:T(1024)(128)(4,1)}), s8[4194304]{0:T(1024)(128)(4,1)S(1)}, s32[]{:S(2)}) async-start(s8[12582912]{0:T(1024)(128)(4,1)} %bitcast.3), calls=%async_computation.4 | async-start | bytes 8388608
  60.3 4.8 %copy-start.3 = (f32[1,12]{1,0:T(1,128)S(1)}, f32[1,12]{1,0:T(1,128)}, u32[]{:S(2)}) copy-start(f32[1,12]{1,0:T(1,128)} %slope_ref.1) | copy-start | bytes 148

commit v3 on v2

--- a/solution.py
+++ b/solution.py
@@ -214,13 +214,35 @@
     )(turned)
 
 
-def inner_kernel(turned_ref, vert_ref, template_ref, vertical_ref, padded, template, written):
+def inner_kernel(turned_ref, vert_ref, vertical_ref, padded):
     rows, width = turned_ref.shape
-    cols = width // LANE
     padded[0:PAD, :] = jnp.zeros((PAD, width - LANE), bf16)
     padded[PAD + rows :, :] = jnp.zeros((LANE - PAD, width - LANE), bf16)
     padded[PAD : PAD + rows, :] = turned_ref[:, LANE:]
 
+    def store(b, at, to, part):
+        vertical_ref[b, at, to] = part
+
+    vertical_step(vert_ref, padded, store)
+
+
+def match_inner(turned, vert):
+    rows, width = turned.shape
+    return pl.pallas_call(
+        inner_kernel,
+        out_shape=jax.ShapeDtypeStruct((vert.shape[0], rows, width - LANE), bf16),
+        in_specs=[vmem(), vmem()],
+        out_specs=vmem(),
+        scratch_shapes=[pltpu.VMEM((rows + LANE, width - LANE), bf16)],
+        cost_estimate=pl.CostEstimate(flops=10**10, bytes_accessed=10**7, transcendentals=0),
+        compiler_params=params(16),
+        name="match_inner",
+    )(turned, vert)
+
+
+def template_kernel(turned_ref, out_ref, done_ref, template_ref, written):
+    rows, width = turned_ref.shape
+    cols = width // LANE
     lane = lax.broadcasted_iota(jnp.int32, (LANE, LANE), 1)
     for n in range(rows // LANE):
         at = slice(n * LANE, (n + 1) * LANE)
@@ -229,40 +251,24 @@
         ]
         for c in range(cols):
             block = jnp.where(lane < LANE - PAD, back[c], back[(c + 1) % cols])
-            template[at, c * LANE : (c + 1) * LANE] = block.astype(bf16)
-    copy = pltpu.make_async_copy(template, template_ref, written)
+            template_ref[at, c * LANE : (c + 1) * LANE] = block.astype(bf16)
+    copy = pltpu.make_async_copy(template_ref, out_ref, written)
     copy.start()
-
-    def store(b, at, to, part):
-        vertical_ref[b, at, to] = part
-
-    @pl.loop(0, 1)
-    def _(_):
-        vertical_step(vert_ref, padded, store)
-
+    done_ref[...] = jnp.zeros(done_ref.shape, f32)
     copy.wait()
 
 
-def match_inner(turned, vert):
-    rows, width = turned.shape
-    hbm = pl.BlockSpec(memory_space=pl.ANY)
-    return pl.pallas_call(
-        inner_kernel,
-        out_shape=(
-            jax.ShapeDtypeStruct((rows, width), bf16),
-            jax.ShapeDtypeStruct((vert.shape[0], rows, width - LANE), bf16),
-        ),
-        in_specs=[vmem(), vmem()],
-        out_specs=(hbm, vmem()),
-        scratch_shapes=[
-            pltpu.VMEM((rows + LANE, width - LANE), bf16),
-            pltpu.VMEM((rows, width), bf16),
-            pltpu.SemaphoreType.DMA,
-        ],
-        cost_estimate=pl.CostEstimate(flops=10**10, bytes_accessed=10**7, transcendentals=0),
+def turn_back(turned):
+    return pl.pallas_call(
+        template_kernel,
+        out_shape=(jax.ShapeDtypeStruct(turned.shape, bf16), jax.ShapeDtypeStruct((8, LANE), f32)),
+        in_specs=[vmem()],
+        out_specs=(pl.BlockSpec(memory_space=pl.ANY), vmem()),
+        scratch_shapes=[pltpu.VMEM(turned.shape, bf16), pltpu.SemaphoreType.DMA],
+        cost_estimate=pl.CostEstimate(flops=10**7, bytes_accessed=4 * 10**6, transcendentals=0),
         compiler_params=params(16),
-        name="match_inner",
-    )(turned, vert)
+        name="template",
+    )(turned)
 
 
 def match_kernel(
@@ -276,6 +282,7 @@
     horiz_ref,
     inner_ref,
     image_ref,
+    _,
     diff_ref,
     padded,
     outer,
@@ -358,12 +365,12 @@
         put(s).wait()
 
 
-def match(counts, index, slopes, turned, low, high, vert, horiz, inner, images, group=GROUP):
+def match(counts, index, slopes, turned, low, high, vert, horiz, inner, images, ahead, group=GROUP):
     slots, rows, width = images.shape
     return pl.pallas_call(
         functools.partial(match_kernel, group=group),
         out_shape=jax.ShapeDtypeStruct(images.shape, bf16),
-        in_specs=[smem()] * 3 + [vmem()] * 7,
+        in_specs=[smem()] * 3 + [vmem()] * 7 + [pl.BlockSpec(memory_space=pl.ANY)],
         out_specs=pl.BlockSpec(memory_space=pl.ANY),
         scratch_shapes=[
             pltpu.VMEM((rows + LANE, 2 * LANE), bf16),
@@ -373,7 +380,7 @@
         ],
         compiler_params=params(24),
         name="match",
-    )(counts, index, slopes, turned, low, high, vert, horiz, inner, images)
+    )(counts, index, slopes, turned, low, high, vert, horiz, inner, images, ahead)
 
 
 def on_device(images, counts, slot_weight, kernel_index, kernel_slope, tap_basis):
@@ -388,11 +395,12 @@
     vert, horiz, held = tap_bands(tap_basis, images)
     ring = [(i, (i + 1) % patches) for i in range(patches)]
     ends = pack_ends(turned)
+    high = lax.ppermute(ends, "patch", [(target, source) for source, target in ring])
     low = lax.ppermute(ends, "patch", ring)
-    high = lax.ppermute(ends, "patch", [(target, source) for source, target in ring])
-    template, inner = match_inner(turned, vert)
+    inner = match_inner(turned, vert)
+    template, done = turn_back(turned)
     differences = match(
-        counts, kernel_index[0], kernel_slope, turned, low, high, vert, horiz, inner, held
+        counts, kernel_index[0], kernel_slope, turned, low, high, vert, horiz, inner, held, done
     )
     return (template, differences)
 

time: 74.7 us -> 73.4 us (0.983)
  waiting for transfers between devices: 6.21 us -> 4.74 us
    ppermute x1, starting transfers between devices: 0.01 us -> 2.87 us  [on_device(): lax.ppermute(ends, 'patch', [(target, source) for source, target in ring])]
    ppermute x1, starting transfers between devices: 5.2 us -> 2.42 us  [on_device(): low = lax.ppermute(ends, 'patch', ring)]
    ppermute x1, waiting for transfers between devices: 1.47 us -> 0.01 us  [on_device(): lax.ppermute(ends, 'patch', [(target, source) for source, target in ring])]
    pallas_call x1 -> x2, Pallas kernels: 3.34 us -> 3.74 us  [the longest x1 2.35 us: match_inner(): pl.pallas_call(inner_kernel, out_shape=jax.ShapeDtypeStruct((vert.shape[0...]
  transfers between devices with their start and end apart: 3 -> 3, of which waited for: 2 -> 1; matrix products, arithmetic and copies ran while one was open for 0% -> 0% of each run, Pallas kernels for 12% -> 13%
where the time goes in v3:
time: 73.4 us; the launch traced here: 72.2 us
  blocking collectives  25.9 us (35%)
  Pallas kernels  23.9 us (33%)
  starting transfers between devices  10.8 us (15%)
  local copies, waits for them, and re-layouts  5.54 us (8%)
  waiting for transfers between devices  4.74 us (6%)
  between operations  1.43 us (2%)
    all_to_all x1, blocking collectives, on_device(): pieces = lax.all_to_all(partial, 'epoch', 0, 0, tiled=True)  25.9 us
    pallas_call x1, Pallas kernels, match(): pl.pallas_call(functools.partial(match_kernel, group=group), out_shape=ja...  8.03 us
    all_to_all x1, starting transfers between devices, on_device(): lax.all_to_all(copies, 'epoch', 0, 0, tiled=True).reshape(rows, width)  5.48 us
    unnamed x16, local copies, waits for them, and re-layouts  5.44 us
    pallas_call x1, Pallas kernels, tap_bands(): pl.pallas_call(bands_kernel, out_shape=(jax.ShapeDtypeStruct((profiles, L...  5.3 us
    pallas_call x1, Pallas kernels, accumulate(): pl.pallas_call(functools.partial(accumulate_kernel, chunk=chunk), out_sha...  5.11 us
    all_to_all x1, waiting for transfers between devices, on_device(): lax.all_to_all(copies, 'epoch', 0, 0, tiled=True).reshape(rows, width)  4.73 us
    ppermute x1, starting transfers between devices, on_device(): lax.ppermute(ends, 'patch', [(target, source) for source, target in ring])  2.87 us
  transfers between devices with their start and end apart: 3, of which 1 were waited for; matrix products, arithmetic and copies ran while one was open for 0% of the time, Pallas kernels for 13%

profile of v3, /device:TPU:9, one launch (start us, length us, event | category | flops | bytes accessed | tf_op | source)
XLA Modules:
  0.0 72.2 jit_solution(14975215471166451788)
XLA Ops:
  0.6 0.0 copy-start.1
  1.3 0.0 copy-start.2
  1.3 0.6 copy-done.2
  2.0 5.1 %accumulate.1 = s32[2304,128]{1,0:T(8,128)S(1)} custom-call(s32[1,1]{1,0:T(1,128)S(6)} %copy.10.counts_ref.count_ref, f32[1,12]{1,0:T(1,128)S(1)} %copy-done.2, bf16[12,512,1024]{2,1,0:T(8,128)(2,1)} %image_ref.3), custom_call_target="tpu_custom_call" | custom-call | tf_op jit(solution)/shard_map/accumulate/pallas_call | solution.py:129
  7.1 25.9 %all_to_all.14.piece_ref = s32[32,72,128]{2,1,0:T(8,128)S(1)} all-to-all(s32[32,72,128]{2,1,0:T(8,128)S(1)} %bitcast.9), channel_id=1, replica_groups=mesh['patch'=4,'epoch'=32] {'epoch'}, dimensions={0} | all-to-all | bytes 2359296 | tf_op jit(solution)/shard_map/all_to_all | solution.py:392
  32.9 1.6 %share.1 = bf16[32,16,1024]{2,1,0:T(8,128)(2,1)} custom-call(s32[32,72,128]{2,1,0:T(8,128)S(1)} %all_to_all.14.piece_ref), custom_call_target="tpu_custom_call" | custom-call | tf_op jit(solution)/shard_map/share/pallas_call | solution.py:173
  34.5 5.5 %all-to-all-start.1 = ((bf16[32,16,1024]{2,1,0:T(8,128)(2,1)}), bf16[32,16,1024]{2,1,0:T(8,128)(2,1)S(1)}, u32[]{:S(2)}, u32[]{:S(2)}) async-start(bf16[32,16,1024]{2,1,0:T(8,128)(2,1)} %share.1), calls=%async_computation.1 | async-start | bytes 2097152 | tf_op jit(solution)/shard_map/all_to_all | solution.py:394
  40.0 0.1 copy.9
  40.1 5.3 %tap_bands.1 = (bf16[8,128,256]{2,1,0:T(8,128)(2,1)S(1)}, bf16[8,256,128]{2,1,0:T(8,128)(2,1)S(1)}, bf16[12,512,1024]{2,1,0:T(8,128)(2,1)S(1)}) custom-call(f32[8,21]{1,0:T(8,128)S(1)} %copy-done.1, bf16[12,512,1024]{2,1,0:T(8,128)(2,1)} %image_ref.3), custom_call_target="tpu_custom_call" | custom-call | tf_op jit(solution)/shard_map/tap_bands/pallas_call | solution.py:62
  45.4 0.0 copy-start
  45.5 4.8 %copy-done = bf16[12,512,1024]{2,1,0:T(8,128)(2,1)} copy-done((bf16[12,512,1024]{2,1,0:T(8,128)(2,1)}, bf16[12,512,1024]{2,1,0:T(8,128)(2,1)S(1)}, u32[]{:S(2)}) %copy-start) | copy-done | bytes 12582936
  50.2 4.7 %all-to-all-done.1 = bf16[32,16,1024]{2,1,0:T(8,128)(2,1)S(1)} async-done(((bf16[32,16,1024]{2,1,0:T(8,128)(2,1)}), bf16[32,16,1024]{2,1,0:T(8,128)(2,1)S(1)}, u32[]{:S(2)}, u32[]{:S(2)}) %all-to-all-start.1) | async-done | bytes 1048608 | tf_op jit(solution)/shard_map/all_to_all | solution.py:394
  55.0 0.1 pack_ends.1
  55.1 2.9 %collective-permute-start.1 = (bf16[128,128]{1,0:T(8,128)(2,1)S(1)}, bf16[128,128]{1,0:T(8,128)(2,1)S(1)}, u32[]{:S(2)}, u32[]{:S(2)}) collective-permute-start(bf16[128,128]{1,0:T(8,128)(2,1)S(1)} %pack_ends.1), channel_id=1, source_target_pairs={{32,0},{64,32},{96,64},{0,96},{33,1},{65,33},{97,65},{1,97},{34,2}... | collective-permute-start | bytes 98312 | tf_op jit(solution)/shard_map/ppermute | solution.py:398
  58.0 2.4 %collective-permute-start = (bf16[128,128]{1,0:T(8,128)(2,1)S(1)}, bf16[128,128]{1,0:T(8,128)(2,1)S(1)}, u32[]{:S(2)}, u32[]{:S(2)}) collective-permute-start(bf16[128,128]{1,0:T(8,128)(2,1)S(1)} %pack_ends.1), channel_id=1, source_target_pairs={{0,32},{32,64},{64,96},{96,0},{1,33},{33,65},{65,97},{97,1},{2,34}... | collective-permute-start | bytes 98312 | tf_op jit(solution)/shard_map/ppermute | solution.py:399
  60.4 2.4 %match_inner.1.inner_ref = bf16[8,512,896]{2,1,0:T(8,128)(2,1)S(1)} custom-call(bf16[512,1024]{1,0:T(8,128)(2,1)S(1)} %bitcast.4, bf16[8,128,256]{2,1,0:T(8,128)(2,1)S(1)} %get-tuple-element.8.vert_ref), custom_call_target="tpu_custom_call" | custom-call | flops 10000000000 | bytes 10000000 | tf_op jit(solution)/shard_map/match_inner/pallas_call | solution.py:231
  62.7 1.4 %template.1 = (bf16[512,1024]{1,0:T(8,128)(2,1)}, f32[8,128]{1,0:T(8,128)S(1)}) custom-call(bf16[512,1024]{1,0:T(8,128)(2,1)S(1)} %bitcast.5), custom_call_target="tpu_custom_call" | custom-call | flops 10000000 | bytes 4000000 | tf_op jit(solution)/shard_map/template/pallas_call | solution.py:262
  64.1 0.0 collective-permute-done.1.high_ref
  64.1 0.0 collective-permute-done.low_ref
  64.2 0.0 slice-done
  64.2 0.0 slice-done.1
  64.2 0.0 slice-done.2
  64.2 0.0 copy-done.3
  64.2 8.0 %match.1 = bf16[12,512,1024]{2,1,0:T(8,128)(2,1)} custom-call(s32[1,1]{1,0:T(1,128)S(6)} %copy.10.counts_ref.count_ref, s32[12,3]{1,0:T(8,128)S(1)} %bitcast.10, f32[1,12]{1,0:T(1,128)S(1)} %copy-done.3, bf16[512,1024]{1,0:T(8,128)(2,1)S(1)} %bitcast.6, bf16[128,128]{1,0:T(8,128)(2,1)S(1)} %collective-permute-done.low_ref, ...), custom_call_target="tpu_custom_call" | custom-call | tf_op jit(solution)/shard_map/match/pallas_call | solution.py:370
  (8 shorter events, 0.0 us)
Async XLA Ops:
  0.6 39.5 %copy-start.1 = (f32[8,21]{1,0:T(8,128)S(1)}, f32[8,21]{1,0:T(8,128)}, u32[]{:S(2)}) copy-start(f32[8,21]{1,0:T(8,128)} %basis_ref.1) | copy-start | bytes 2020
  1.3 0.7 copy-start.2
  2.0 38.1 %copy-start.4 = (s32[1,12,3]{1,0,2:T(1,128)S(1)}, s32[1,12,3]{1,0,2:T(1,128)}, u32[]{:S(2)}) copy-start(s32[1,12,3]{1,0,2:T(1,128)} %param.9) | copy-start | bytes 436
  34.5 20.4 %all-to-all-start.1 = ((bf16[32,16,1024]{2,1,0:T(8,128)(2,1)}), bf16[32,16,1024]{2,1,0:T(8,128)(2,1)S(1)}, u32[]{:S(2)}, u32[]{:S(2)}) async-start(bf16[32,16,1024]{2,1,0:T(8,128)(2,1)} %share.1), calls=%async_computation.1 | async-start | bytes 2097152 | tf_op jit(solution)/shard_map/all_to_all | solution.py:394
  45.4 4.8 %copy-start = (bf16[12,512,1024]{2,1,0:T(8,128)(2,1)}, bf16[12,512,1024]{2,1,0:T(8,128)(2,1)S(1)}, u32[]{:S(2)}) copy-start(bf16[12,512,1024]{2,1,0:T(8,128)(2,1)S(1)} %get-tuple-element.10.image_ref) | copy-start | bytes 37748740
  55.0 9.2 %slice-start = ((s8[12582912]{0:T(1024)(128)(4,1)}), s8[4194304]{0:T(1024)(128)(4,1)S(1)}, s32[]{:S(2)}) async-start(s8[12582912]{0:T(1024)(128)(4,1)} %bitcast.7), calls=%async_computation.2 | async-start | bytes 8388608
  55.1 9.0 %collective-permute-start.1 = (bf16[128,128]{1,0:T(8,128)(2,1)S(1)}, bf16[128,128]{1,0:T(8,128)(2,1)S(1)}, u32[]{:S(2)}, u32[]{:S(2)}) collective-permute-start(bf16[128,128]{1,0:T(8,128)(2,1)S(1)} %pack_ends.1), channel_id=1, source_target_pairs={{32,0},{64,32},{96,64},{0,96},{33,1},{65,33},{97,65},{1,97},{34,2}... | collective-permute-start | bytes 98312 | tf_op jit(solution)/shard_map/ppermute | solution.py:398
  58.0 6.2 %collective-permute-start = (bf16[128,128]{1,0:T(8,128)(2,1)S(1)}, bf16[128,128]{1,0:T(8,128)(2,1)S(1)}, u32[]{:S(2)}, u32[]{:S(2)}) collective-permute-start(bf16[128,128]{1,0:T(8,128)(2,1)S(1)} %pack_ends.1), channel_id=1, source_target_pairs={{0,32},{32,64},{64,96},{96,0},{1,33},{33,65},{65,97},{97,1},{2,34}... | collective-permute-start | bytes 98312 | tf_op jit(solution)/shard_map/ppermute | solution.py:399
  60.4 3.8 %slice-start.1 = ((s8[12582912]{0:T(1024)(128)(4,1)}), s8[4194304]{0:T(1024)(128)(4,1)S(1)}, s32[]{:S(2)}) async-start(s8[12582912]{0:T(1024)(128)(4,1)} %bitcast.7), calls=%async_computation.3 | async-start | bytes 8388608
  60.4 3.8 %slice-start.2 = ((s8[12582912]{0:T(1024)(128)(4,1)}), s8[4194304]{0:T(1024)(128)(4,1)S(1)}, s32[]{:S(2)}) async-start(s8[12582912]{0:T(1024)(128)(4,1)} %bitcast.7), calls=%async_computation.4 | async-start | bytes 8388608
  60.4 3.8 %copy-start.3 = (f32[1,12]{1,0:T(1,128)S(1)}, f32[1,12]{1,0:T(1,128)}, u32[]{:S(2)}) copy-start(f32[1,12]{1,0:T(1,128)} %slope_ref.1) | copy-start | bytes 148

commit v4 on v3

--- a/solution.py
+++ b/solution.py
@@ -124,7 +124,7 @@
             pack(upper + lower, weight_word, out_ref, (n * (block // chunk) + q) * stride)
 
 
-def accumulate(counts, weight, images, chunk=16, block=64):
+def accumulate(counts, weight, images, chunk=16, block=32):
     slots, rows, width = images.shape
     return pl.pallas_call(
         functools.partial(accumulate_kernel, chunk=chunk),
@@ -316,13 +316,9 @@
             padded[at, LANE:] = jnp.where(lane < PAD, own, right).astype(bf16)
 
         def store(b, at, _, part):
-            outer[b, at, :LANE] = part[:, :LANE]
-            outer[b, at, 3 * LANE :] = part[:, LANE:]
+            outer[b, at, :] = part
 
         vertical_step(vert_ref, padded, store)
-        for b in range(vert_ref.shape[0]):
-            outer[b, :, LANE : 2 * LANE] = inner_ref[b, :, :LANE]
-            outer[b, :, 2 * LANE : 3 * LANE] = inner_ref[b, :, width - 2 * LANE :]
 
     center = width * lax.axis_size("patch") / 2
     column = lax.broadcasted_iota(jnp.int32, (8, LANE), 1) + patch * width
@@ -339,9 +335,11 @@
                 for m in range(cols):
                     at = slice(m * LANE, (m + 1) * LANE)
                     if m == 0:
-                        window = outer[first, :, : 2 * LANE]
+                        window = jnp.concatenate([outer[first, :, :LANE], inner_ref[first, :, :LANE]], axis=1)
                     elif m == cols - 1:
-                        window = outer[first, :, 2 * LANE :]
+                        window = jnp.concatenate(
+                            [inner_ref[first, :, width - 2 * LANE :], outer[first, :, LANE:]], axis=1
+                        )
                     else:
                         window = inner_ref[first, :, (m - 1) * LANE : (m + 1) * LANE]
                     position = ((column + m * LANE).astype(f32) + 0.5 - center) / center
@@ -374,7 +372,7 @@
         out_specs=pl.BlockSpec(memory_space=pl.ANY),
         scratch_shapes=[
             pltpu.VMEM((rows + LANE, 2 * LANE), bf16),
-            pltpu.VMEM((vert.shape[0], rows, 4 * LANE), bf16),
+            pltpu.VMEM((vert.shape[0], rows, 2 * LANE), bf16),
             pltpu.VMEM(images.shape, bf16),
             pltpu.SemaphoreType.DMA((slots,)),
         ],

time: 73.4 us -> 73.2 us (level); the launches traced: 72.2 us -> 73 us
  Pallas kernels: 23.9 us -> 24.7 us
    pallas_call x1, Pallas kernels: 8.03 us -> 8.97 us  [match(): pl.pallas_call(functools.partial(match_kernel, group=group), out_shape=ja...]
  transfers between devices with their start and end apart: 3 -> 3, of which waited for: 1 -> 1; matrix products, arithmetic and copies ran while one was open for 0% -> 0% of each run, Pallas kernels for 13% -> 12%
where the time goes in v4:
time: 73.2 us; the launch traced here: 73 us
  blocking collectives  25.9 us (35%)
  Pallas kernels  24.7 us (34%)
  starting transfers between devices  10.8 us (15%)
  local copies, waits for them, and re-layouts  5.54 us (8%)
  waiting for transfers between devices  4.74 us (6%)
  between operations  1.43 us (2%)
    all_to_all x1, blocking collectives, on_device(): pieces = lax.all_to_all(partial, 'epoch', 0, 0, tiled=True)  25.9 us
    pallas_call x1, Pallas kernels, match(): pl.pallas_call(functools.partial(match_kernel, group=group), out_shape=ja...  8.97 us
    all_to_all x1, starting transfers between devices, on_device(): lax.all_to_all(copies, 'epoch', 0, 0, tiled=True).reshape(rows, width)  5.48 us
    unnamed x16, local copies, waits for them, and re-layouts  5.44 us
    pallas_call x1, Pallas kernels, tap_bands(): pl.pallas_call(bands_kernel, out_shape=(jax.ShapeDtypeStruct((profiles, L...  5.3 us
    pallas_call x1, Pallas kernels, accumulate(): pl.pallas_call(functools.partial(accumulate_kernel, chunk=chunk), out_sha...  4.94 us
    all_to_all x1, waiting for transfers between devices, on_device(): lax.all_to_all(copies, 'epoch', 0, 0, tiled=True).reshape(rows, width)  4.73 us
    ppermute x1, starting transfers between devices, on_device(): lax.ppermute(ends, 'patch', [(target, source) for source, target in ring])  2.87 us
  transfers between devices with their start and end apart: 3, of which 1 were waited for; matrix products, arithmetic and copies ran while one was open for 0% of the time, Pallas kernels for 12%

profile of v4, /device:TPU:9, one launch (start us, length us, event | category | flops | bytes accessed | tf_op | source)
XLA Modules:
  0.0 73.0 jit_solution(9550112624741440659)
XLA Ops:
  0.6 0.0 copy-start.1
  1.3 0.0 copy-start.2
  1.3 0.6 copy-done.2
  2.0 4.9 %accumulate.1 = s32[2304,128]{1,0:T(8,128)S(1)} custom-call(s32[1,1]{1,0:T(1,128)S(6)} %copy.10.counts_ref.count_ref, f32[1,12]{1,0:T(1,128)S(1)} %copy-done.2, bf16[12,512,1024]{2,1,0:T(8,128)(2,1)} %image_ref.3), custom_call_target="tpu_custom_call" | custom-call | tf_op jit(solution)/shard_map/accumulate/pallas_call | solution.py:129
  6.9 25.9 %all_to_all.14.piece_ref = s32[32,72,128]{2,1,0:T(8,128)S(1)} all-to-all(s32[32,72,128]{2,1,0:T(8,128)S(1)} %bitcast.9), channel_id=1, replica_groups=mesh['patch'=4,'epoch'=32] {'epoch'}, dimensions={0} | all-to-all | bytes 2359296 | tf_op jit(solution)/shard_map/all_to_all | solution.py:390
  32.8 1.6 %share.1 = bf16[32,16,1024]{2,1,0:T(8,128)(2,1)} custom-call(s32[32,72,128]{2,1,0:T(8,128)S(1)} %all_to_all.14.piece_ref), custom_call_target="tpu_custom_call" | custom-call | tf_op jit(solution)/shard_map/share/pallas_call | solution.py:173
  34.4 5.5 %all-to-all-start.1 = ((bf16[32,16,1024]{2,1,0:T(8,128)(2,1)}), bf16[32,16,1024]{2,1,0:T(8,128)(2,1)S(1)}, u32[]{:S(2)}, u32[]{:S(2)}) async-start(bf16[32,16,1024]{2,1,0:T(8,128)(2,1)} %share.1), calls=%async_computation.1 | async-start | bytes 2097152 | tf_op jit(solution)/shard_map/all_to_all | solution.py:392
  39.9 0.0 copy-done.4
  39.9 0.1 copy.9
  40.0 0.0 copy-done.1
  40.0 5.3 %tap_bands.1 = (bf16[8,128,256]{2,1,0:T(8,128)(2,1)S(1)}, bf16[8,256,128]{2,1,0:T(8,128)(2,1)S(1)}, bf16[12,512,1024]{2,1,0:T(8,128)(2,1)S(1)}) custom-call(f32[8,21]{1,0:T(8,128)S(1)} %copy-done.1, bf16[12,512,1024]{2,1,0:T(8,128)(2,1)} %image_ref.3), custom_call_target="tpu_custom_call" | custom-call | tf_op jit(solution)/shard_map/tap_bands/pallas_call | solution.py:62
  45.3 0.0 copy-start
  45.3 4.8 %copy-done = bf16[12,512,1024]{2,1,0:T(8,128)(2,1)} copy-done((bf16[12,512,1024]{2,1,0:T(8,128)(2,1)}, bf16[12,512,1024]{2,1,0:T(8,128)(2,1)S(1)}, u32[]{:S(2)}) %copy-start) | copy-done | bytes 12582936
  50.1 4.7 %all-to-all-done.1 = bf16[32,16,1024]{2,1,0:T(8,128)(2,1)S(1)} async-done(((bf16[32,16,1024]{2,1,0:T(8,128)(2,1)}), bf16[32,16,1024]{2,1,0:T(8,128)(2,1)S(1)}, u32[]{:S(2)}, u32[]{:S(2)}) %all-to-all-start.1) | async-done | bytes 1048608 | tf_op jit(solution)/shard_map/all_to_all | solution.py:392
  54.8 0.1 pack_ends.1
  54.9 2.9 %collective-permute-start.1 = (bf16[128,128]{1,0:T(8,128)(2,1)S(1)}, bf16[128,128]{1,0:T(8,128)(2,1)S(1)}, u32[]{:S(2)}, u32[]{:S(2)}) collective-permute-start(bf16[128,128]{1,0:T(8,128)(2,1)S(1)} %pack_ends.1), channel_id=1, source_target_pairs={{32,0},{64,32},{96,64},{0,96},{33,1},{65,33},{97,65},{1,97},{34,2}... | collective-permute-start | bytes 98312 | tf_op jit(solution)/shard_map/ppermute | solution.py:396
  57.8 2.4 %collective-permute-start = (bf16[128,128]{1,0:T(8,128)(2,1)S(1)}, bf16[128,128]{1,0:T(8,128)(2,1)S(1)}, u32[]{:S(2)}, u32[]{:S(2)}) collective-permute-start(bf16[128,128]{1,0:T(8,128)(2,1)S(1)} %pack_ends.1), channel_id=1, source_target_pairs={{0,32},{32,64},{64,96},{96,0},{1,33},{33,65},{65,97},{97,1},{2,34}... | collective-permute-start | bytes 98312 | tf_op jit(solution)/shard_map/ppermute | solution.py:397
  60.2 2.4 %match_inner.1.inner_ref = bf16[8,512,896]{2,1,0:T(8,128)(2,1)S(1)} custom-call(bf16[512,1024]{1,0:T(8,128)(2,1)S(1)} %bitcast.4, bf16[8,128,256]{2,1,0:T(8,128)(2,1)S(1)} %get-tuple-element.8.vert_ref), custom_call_target="tpu_custom_call" | custom-call | flops 10000000000 | bytes 10000000 | tf_op jit(solution)/shard_map/match_inner/pallas_call | solution.py:231
  62.6 1.4 %template.1 = (bf16[512,1024]{1,0:T(8,128)(2,1)}, f32[8,128]{1,0:T(8,128)S(1)}) custom-call(bf16[512,1024]{1,0:T(8,128)(2,1)S(1)} %bitcast.5), custom_call_target="tpu_custom_call" | custom-call | flops 10000000 | bytes 4000000 | tf_op jit(solution)/shard_map/template/pallas_call | solution.py:262
  64.0 0.0 collective-permute-done.1.high_ref
  64.0 0.0 collective-permute-done.low_ref
  64.0 0.0 slice-done
  64.0 0.0 slice-done.1
  64.0 9.0 %match.1 = bf16[12,512,1024]{2,1,0:T(8,128)(2,1)} custom-call(s32[1,1]{1,0:T(1,128)S(6)} %copy.10.counts_ref.count_ref, s32[12,3]{1,0:T(8,128)S(1)} %bitcast.10, f32[1,12]{1,0:T(1,128)S(1)} %copy-done.3, bf16[512,1024]{1,0:T(8,128)(2,1)S(1)} %bitcast.6, bf16[128,128]{1,0:T(8,128)(2,1)S(1)} %collective-permute-done.low_ref, ...), custom_call_target="tpu_custom_call" | custom-call | tf_op jit(solution)/shard_map/match/pallas_call | solution.py:368
  (8 shorter events, 0.0 us)
Async XLA Ops:
  0.6 39.3 %copy-start.1 = (f32[8,21]{1,0:T(8,128)S(1)}, f32[8,21]{1,0:T(8,128)}, u32[]{:S(2)}) copy-start(f32[8,21]{1,0:T(8,128)} %basis_ref.1) | copy-start | bytes 2020
  1.3 0.7 copy-start.2
  2.0 37.9 %copy-start.4 = (s32[1,12,3]{1,0,2:T(1,128)S(1)}, s32[1,12,3]{1,0,2:T(1,128)}, u32[]{:S(2)}) copy-start(s32[1,12,3]{1,0,2:T(1,128)} %param.9) | copy-start | bytes 436
  34.4 20.4 %all-to-all-start.1 = ((bf16[32,16,1024]{2,1,0:T(8,128)(2,1)}), bf16[32,16,1024]{2,1,0:T(8,128)(2,1)S(1)}, u32[]{:S(2)}, u32[]{:S(2)}) async-start(bf16[32,16,1024]{2,1,0:T(8,128)(2,1)} %share.1), calls=%async_computation.1 | async-start | bytes 2097152 | tf_op jit(solution)/shard_map/all_to_all | solution.py:392
  45.3 4.8 %copy-start = (bf16[12,512,1024]{2,1,0:T(8,128)(2,1)}, bf16[12,512,1024]{2,1,0:T(8,128)(2,1)S(1)}, u32[]{:S(2)}) copy-start(bf16[12,512,1024]{2,1,0:T(8,128)(2,1)S(1)} %get-tuple-element.10.image_ref) | copy-start | bytes 37748740
  54.8 9.2 %slice-start = ((s8[12582912]{0:T(1024)(128)(4,1)}), s8[4194304]{0:T(1024)(128)(4,1)S(1)}, s32[]{:S(2)}) async-start(s8[12582912]{0:T(1024)(128)(4,1)} %bitcast.7), calls=%async_computation.2 | async-start | bytes 8388608
  54.9 9.0 %collective-permute-start.1 = (bf16[128,128]{1,0:T(8,128)(2,1)S(1)}, bf16[128,128]{1,0:T(8,128)(2,1)S(1)}, u32[]{:S(2)}, u32[]{:S(2)}) collective-permute-start(bf16[128,128]{1,0:T(8,128)(2,1)S(1)} %pack_ends.1), channel_id=1, source_target_pairs={{32,0},{64,32},{96,64},{0,96},{33,1},{65,33},{97,65},{1,97},{34,2}... | collective-permute-start | bytes 98312 | tf_op jit(solution)/shard_map/ppermute | solution.py:396
  57.8 6.2 %collective-permute-start = (bf16[128,128]{1,0:T(8,128)(2,1)S(1)}, bf16[128,128]{1,0:T(8,128)(2,1)S(1)}, u32[]{:S(2)}, u32[]{:S(2)}) collective-permute-start(bf16[128,128]{1,0:T(8,128)(2,1)S(1)} %pack_ends.1), channel_id=1, source_target_pairs={{0,32},{32,64},{64,96},{96,0},{1,33},{33,65},{65,97},{97,1},{2,34}... | collective-permute-start | bytes 98312 | tf_op jit(solution)/shard_map/ppermute | solution.py:397
  60.2 3.8 %slice-start.1 = ((s8[12582912]{0:T(1024)(128)(4,1)}), s8[4194304]{0:T(1024)(128)(4,1)S(1)}, s32[]{:S(2)}) async-start(s8[12582912]{0:T(1024)(128)(4,1)} %bitcast.7), calls=%async_computation.3 | async-start | bytes 8388608
  60.2 3.8 %slice-start.2 = ((s8[12582912]{0:T(1024)(128)(4,1)}), s8[4194304]{0:T(1024)(128)(4,1)S(1)}, s32[]{:S(2)}) async-start(s8[12582912]{0:T(1024)(128)(4,1)} %bitcast.7), calls=%async_computation.4 | async-start | bytes 8388608
  60.2 3.8 %copy-start.3 = (f32[1,12]{1,0:T(1,128)S(1)}, f32[1,12]{1,0:T(1,128)}, u32[]{:S(2)}) copy-start(f32[1,12]{1,0:T(1,128)} %slope_ref.1) | copy-start | bytes 148
